TPU v7x, 256 devices: a whole 4x4x8 slice. The times are simulated.
256 devices in a mesh: cls: 32 (over x, y, core), feat: 8 (over z).
Axes of the slice: x: 4, y: 4, z: 8, core: 2. Of those that a mesh axis runs over, the one named last changes fastest.
Arguments:
- hidden_states: bfloat16 [512, 4096], P(None, 'feat'), may hold values from -24 to 24
- weight: bfloat16 [131072, 4096], P('cls', 'feat'), may hold values from -0.87890625 to 0.87890625
- target: int32 [512], replicated, may hold values from 0 to 131071
- row_moment: float32 [131072], P('cls'), may hold values from 1e-14 to 0.01
- col_moment: float32 [4096], P('feat'), may hold values from 0.002 to 0.008
Outputs:
- input_grad: bfloat16 [512, 4096], P(None, 'feat')
- row_loss: float32 [512], P('feat')
- new_weight: bfloat16 [131072, 4096], P('cls', 'feat')
- new_row_moment: float32 [131072], P('cls')
- new_col_moment: float32 [4096], P('feat')
All inputs are finite; a program needn't handle non-finite values.
Results may differ from a plain program's by a relative error of at most 0.0004.
The roundings to bfloat16 on the way count: a program that leaves them out, or rounds other values in their place, can miss the bound.
Values may be sent and summed in bfloat16 or wider, within the bound.
A program may use at most 128 MiB of HBM per device.

v0:
```python
import jax
import jax.numpy as jnp
from jax import lax
from jax.sharding import PartitionSpec as P

D = 4096
V = 131072


tiny_square = 1e-30
decay_rate = 0.4
step_size = 0.1
clip_limit = 0.1


def on_device(hidden_states, weight, target, row_moment, col_moment):
    feat_count = lax.axis_size("feat")
    share_rows = hidden_states.shape[0] // feat_count
    local_classes = weight.shape[0]
    class_start = lax.axis_index("cls") * local_classes
    row_offset = lax.axis_index("feat") * share_rows
    contract_feat = (((1,), (1,)), ((), ()))
    partial_value = lax.dot_general(
        hidden_states, weight, contract_feat, preferred_element_type=jnp.float32
    )
    logits = lax.psum(partial_value, "feat")
    columns = lax.broadcasted_iota(jnp.int32, (1, local_classes), 1) + class_start
    target_mask = columns == target[:, None]
    local_picked = jnp.sum(jnp.where(target_mask, logits, jnp.float32(0.0)), axis=1)
    row_top = lax.pmax(jnp.max(logits, axis=1), "cls")
    shifted = jnp.exp(logits - row_top[:, None])
    exp_total, picked = lax.psum((jnp.sum(shifted, axis=1), local_picked), "cls")
    row_loss = jnp.log(exp_total) + row_top - picked
    dlogits = (shifted / exp_total[:, None] - target_mask.astype(jnp.float32)).astype(jnp.bfloat16)
    own_loss = lax.dynamic_slice_in_dim(row_loss, row_offset, share_rows, 0)
    input_part = jnp.dot(dlogits, weight, preferred_element_type=jnp.float32)
    weight_grad = lax.dot_general(
        dlogits, hidden_states, (((0,), (0,)), ((), ())), preferred_element_type=jnp.float32
    )
    squares = weight_grad * weight_grad + tiny_square
    input_sum, col_sum = lax.psum((input_part, jnp.sum(squares, axis=0)), "cls")
    input_grad = input_sum.astype(jnp.bfloat16)
    row_sum = lax.psum(jnp.sum(squares, axis=1), "feat")
    new_row_moment = decay_rate * row_moment + (1.0 - decay_rate) * (row_sum / D)
    new_col_moment = decay_rate * col_moment + (1.0 - decay_rate) * (col_sum / V)
    update = weight_grad * lax.rsqrt(new_row_moment[:, None] * new_col_moment[None, :])
    update_square = lax.psum(jnp.sum(update * update), ("cls", "feat"))
    update_rms = jnp.sqrt(update_square / (V * D))
    clip_scale = 1.0 / jnp.maximum(jnp.float32(1.0), update_rms / clip_limit)
    new_weight = (weight.astype(jnp.float32) - step_size * clip_scale * update).astype(jnp.bfloat16)
    return (input_grad, own_loss, new_weight, new_row_moment, new_col_moment)


def solution(mesh):
    placed = (P(None, "feat"), P("cls", "feat"), P(), P("cls"), P("feat"))
    return jax.shard_map(
        on_device,
        mesh=mesh,
        in_specs=placed,
        out_specs=(P(None, "feat"), P("feat"), P("cls", "feat"), P("cls"), P("feat")),
        check_vma=False,
    )
```

profile of v0, /device:TPU:1, one launch (start us, length us, event | category | flops | bytes accessed | tf_op | source)
XLA Modules:
  0.0 616.2 jit_solution(10610031307792776548)
XLA Ops:
  7.2 0.0 copy-start
  7.2 0.0 all-reduce.4.cloned.1.call-start
  7.2 1.0 copy-done
  8.2 7.8 %fusion.6 = f32[512,4096]{1,0:T(8,128)} fusion(bf16[512,512]{1,0:T(8,128)(2,1)S(1)} %copy-done, bf16[4096,512]{1,0:T(8,128)(2,1)} %param.6), kind=kOutput, calls=%fused_computation.17 | convolution fusion | flops 2147483648 | bytes 13107200 | tf_op jit(solution)/shard_map/dot_general | solution.py:23
  16.0 0.0 copy-start.5
  16.0 0.0 all-reduce.4.cloned.1.call-update
  16.0 192.0 %all-reduce.4.cloned.1.call-done = f32[512,4096]{1,0:T(8,128)} async-done(((f32[512,4096]{1,0:T(8,128)}), f32[512,4096]{1,0:T(8,128)}) %all-reduce.4.cloned.1.call-update) | async-done | bytes 8388624 | tf_op jit(solution)/shard_map/psum | solution.py:26
  208.0 3.8 reduce_max.9
  211.9 62.7 %pmax.7 = f32[512]{0:T(512)S(1)} all-reduce(f32[512]{0:T(512)S(1)} %reduce_max.9), channel_id=1, replica_groups=mesh['cls'=32,'feat'=8] {'cls'}, use_global_device_ids=true, to_apply=%region_2.3 | all-reduce | flops 512 | bytes 4096 | tf_op jit(solution)/shard_map/pmax | solution.py:30
  274.6 0.0 copy-done.5
  274.6 4.7 fusion.2
  279.3 67.0 %psum.50 = f32[512]{0:T(512)S(1)} all-reduce(f32[512]{0:T(512)S(1)} %get-tuple-element.8), channel_id=1, replica_groups=mesh['cls'=32,'feat'=8] {'cls'}, use_global_device_ids=true, to_apply=%region_4.5 | all-reduce | flops 512 | bytes 4096 | tf_op jit(solution)/shard_map/psum | solution.py:32
  346.3 5.1 fusion.1
  351.4 0.0 copy-start.1
  351.4 6.0 fusion.5
  357.4 0.0 copy-done.1
  357.5 0.0 copy-start.6
  357.5 0.0 copy-start.4
  357.5 2.3 fusion.7
  359.8 21.2 %psum.53 = f32[4096]{0:T(1024)S(1)} all-reduce(f32[4096]{0:T(1024)S(1)} %get-tuple-element.5), channel_id=1, replica_groups=mesh['cls'=32,'feat'=8] {'feat'}, use_global_device_ids=true, to_apply=%region_9.10 | all-reduce | flops 4096 | bytes 32768 | tf_op jit(solution)/shard_map/psum | solution.py:43
  381.0 138.1 %all-reduce.5 = (bf16[512,512]{1,0:T(8,128)(2,1)}, f32[512]{0:T(512)S(1)}, f32[512]{0:T(512)S(1)}) all-reduce(f32[512,512]{1,0:T(8,128)S(1)} %fusion.7, f32[512]{0:T(512)S(1)} %get-tuple-element.7, f32[512]{0:T(512)S(1)} %get-tuple-element.6), channel_id=1, replica_groups=mesh['cls'=32,'feat'=8] {'cls'}, use_global_device_ids=true, to_apply=%region_5.6 | all-reduce | flops 263168 | bytes 1581056 | tf_op jit(solution)/shard_map/psum | solution.py:41
  519.1 0.0 copy-done.6
  519.1 0.0 copy-done.4
  519.1 0.0 copy-start.3
  519.1 0.0 copy-start.2
  519.2 5.6 multiply_reduce_fusion
  524.7 76.3 %psum.55 = f32[]{:T(128)} all-reduce(f32[]{:T(128)} %multiply_reduce_fusion), channel_id=1, replica_groups=mesh['cls'=32,'feat'=8] {'cls','feat'}, use_global_device_ids=true, to_apply=%region_13.14 | all-reduce | flops 1 | bytes 8 | tf_op jit(solution)/shard_map/psum | solution.py:47
  601.8 6.9 %subtract_convert_fusion = bf16[4096,512]{1,0:T(8,128)(2,1)} fusion(bf16[4096,512]{1,0:T(8,128)(2,1)} %param.6, f32[4096,512]{1,0:T(8,128)} %get-tuple-element.12, f32[]{:T(128)S(6)} %mul.77, f32[512]{0:T(512)S(1)} %multiply_add_fusion.2, f32[4096]{0:T(1024)S(1)} %multiply_add_fusion.1), kind=kLoop, calls=%fused_computation.5 | loop fusion | flops 12582912 | bytes 16795652 | tf_op jit(solution)/shard_map/convert_element_type | solution.py:50
  608.7 0.0 copy-done.3
  608.7 0.0 copy-done.2
  608.7 0.6 dynamic_slice.3
  (4 shorter events, 0.0 us)
Async XLA Ops:
  7.2 1.0 copy-start
  7.2 200.8 %all-reduce.4.cloned.1.call-start = ((), (), s32[]{:S(2)}) async-start(), calls=%async_computation | async-start | bytes 16777216 | tf_op jit(solution)/shard_map/psum | solution.py:26
  16.0 258.6 %copy-start.5 = (s32[512]{0:T(512)S(1)}, s32[512]{0:T(512)}, u32[]{:S(2)}) copy-start(s32[512]{0:T(512)} %param.7) | copy-start | bytes 6148
  351.4 6.0 copy-start.1
  357.5 161.7 %copy-start.6 = (f32[512]{0:T(512)S(1)}, f32[512]{0:T(512)}, u32[]{:S(2)}) copy-start(f32[512]{0:T(512)} %param.9) | copy-start | bytes 6148
  357.5 161.7 %copy-start.4 = (f32[4096]{0:T(1024)S(1)}, f32[4096]{0:T(1024)}, u32[]{:S(2)}) copy-start(f32[4096]{0:T(1024)} %param.8) | copy-start | bytes 49156
  519.1 89.6 %copy-start.3 = (f32[512]{0:T(512)}, f32[512]{0:T(512)S(1)}, u32[]{:S(2)}) copy-start(f32[512]{0:T(512)S(1)} %multiply_add_fusion.2) | copy-start | bytes 6148
  519.1 89.6 %copy-start.2 = (f32[4096]{0:T(1024)}, f32[4096]{0:T(1024)S(1)}, u32[]{:S(2)}) copy-start(f32[4096]{0:T(1024)S(1)} %multiply_add_fusion.1) | copy-start | bytes 49156
Sparse Core Ops, SparseCore 0:
  16.1 191.8 all-reduce.3
where the time goes:
time: 617 us; the launch traced here: 616 us
  blocking collectives  365 us (59%)
  waiting for transfers between devices  192 us (31%)
  other arithmetic  26.2 us (4%)
  matrix products  16.1 us (3%)
  between operations  14.8 us (2%)
    psum x1, waiting for transfers between devices, on_device(): logits = lax.psum(partial_value, 'feat')  192 us
    psum x1, blocking collectives, on_device(): input_sum, col_sum = lax.psum((input_part, jnp.sum(squares, axis=0)), 'cls')  138 us
    psum x1, blocking collectives, on_device(): update_square = lax.psum(jnp.sum(update * update), ('cls', 'feat'))  76.3 us
    psum x1, blocking collectives, on_device(): lax.psum((jnp.sum(shifted, axis=1), local_picked), 'cls')  67 us
    pmax x1, blocking collectives, on_device(): row_top = lax.pmax(jnp.max(logits, axis=1), 'cls')  62.7 us
    psum x1, blocking collectives, on_device(): row_sum = lax.psum(jnp.sum(squares, axis=1), 'feat')  21.2 us
  transfers between devices with their start and end apart: 1, of which 1 were waited for; matrix products, arithmetic and copies ran while one was open for 0% of the time, Pallas kernels for 0%

commit v1 on v0

--- a/solution.py
+++ b/solution.py
@@ -17,26 +17,27 @@
     feat_count = lax.axis_size("feat")
     share_rows = hidden_states.shape[0] // feat_count
     local_classes = weight.shape[0]
-    class_start = lax.axis_index("cls") * local_classes
+    own_classes = local_classes // feat_count
+    class_start = lax.axis_index("cls") * local_classes + lax.axis_index("feat") * own_classes
     row_offset = lax.axis_index("feat") * share_rows
-    contract_feat = (((1,), (1,)), ((), ()))
     partial_value = lax.dot_general(
-        hidden_states, weight, contract_feat, preferred_element_type=jnp.float32
+        weight, hidden_states, (((1,), (1,)), ((), ())), preferred_element_type=jnp.float32
     )
-    logits = lax.psum(partial_value, "feat")
-    columns = lax.broadcasted_iota(jnp.int32, (1, local_classes), 1) + class_start
-    target_mask = columns == target[:, None]
-    local_picked = jnp.sum(jnp.where(target_mask, logits, jnp.float32(0.0)), axis=1)
-    row_top = lax.pmax(jnp.max(logits, axis=1), "cls")
-    shifted = jnp.exp(logits - row_top[:, None])
-    exp_total, picked = lax.psum((jnp.sum(shifted, axis=1), local_picked), "cls")
+    logits = lax.psum_scatter(partial_value, "feat", scatter_dimension=0, tiled=True)
+    classes = lax.broadcasted_iota(jnp.int32, (own_classes, 1), 0) + class_start
+    target_mask = classes == target[None, :]
+    local_picked = jnp.sum(jnp.where(target_mask, logits, jnp.float32(0.0)), axis=0)
+    row_top = lax.pmax(jnp.max(logits, axis=0), ("cls", "feat"))
+    shifted = jnp.exp(logits - row_top[None, :])
+    exp_total, picked = lax.psum((jnp.sum(shifted, axis=0), local_picked), ("cls", "feat"))
     row_loss = jnp.log(exp_total) + row_top - picked
-    dlogits = (shifted / exp_total[:, None] - target_mask.astype(jnp.float32)).astype(jnp.bfloat16)
+    own_dlogits = (shifted / exp_total[None, :] - target_mask.astype(jnp.float32)).astype(jnp.bfloat16)
+    dlogits = lax.all_gather(own_dlogits, "feat", axis=0, tiled=True)
     own_loss = lax.dynamic_slice_in_dim(row_loss, row_offset, share_rows, 0)
-    input_part = jnp.dot(dlogits, weight, preferred_element_type=jnp.float32)
-    weight_grad = lax.dot_general(
-        dlogits, hidden_states, (((0,), (0,)), ((), ())), preferred_element_type=jnp.float32
+    input_part = lax.dot_general(
+        dlogits, weight, (((0,), (0,)), ((), ())), preferred_element_type=jnp.float32
     )
+    weight_grad = jnp.dot(dlogits, hidden_states, preferred_element_type=jnp.float32)
     squares = weight_grad * weight_grad + tiny_square
     input_sum, col_sum = lax.psum((input_part, jnp.sum(squares, axis=0)), "cls")
     input_grad = input_sum.astype(jnp.bfloat16)

time: 617 us -> 589 us (0.955)
  waiting for transfers between devices: 192 us -> 151 us
  blocking collectives: 365 us -> 384 us
  other arithmetic: 26.2 us -> 17.6 us
    psum x1 -> x0, waiting for transfers between devices: 192 us -> none  [on_device(): logits = lax.psum(partial_value, 'feat')]
    reduce_scatter x0 -> x1, waiting for transfers between devices: none -> 98.9 us  [on_device(): lax.psum_scatter(partial_value, 'feat', scatter_dimension=0, tiled=True)]
    all_gather x0 -> x1, waiting for transfers between devices: none -> 51.6 us  [on_device(): dlogits = lax.all_gather(own_dlogits, 'feat', axis=0, tiled=True)]
    pmax x1, blocking collectives: 62.7 us -> 76.4 us  [on_device(): row_top = lax.pmax(jnp.max(logits, axis=0), ('cls', 'feat'))]
  transfers between devices with their start and end apart: 1 -> 2, of which waited for: 1 -> 2; matrix products, arithmetic and copies ran while one was open for 0% -> 0% of each run, Pallas kernels for 0% -> 0%
where the time goes in v1:
time: 589 us
  blocking collectives  384 us (65%)
  waiting for transfers between devices  151 us (26%)
  matrix products  19.7 us (3%)
  other arithmetic  17.6 us (3%)
  between operations  14.9 us (3%)
    psum x2, blocking collectives, on_device(): lax.psum((jnp.sum(shifted, axis=0), local_picked), ('cls', 'feat'))  149 us
    psum x1, blocking collectives, on_device(): input_sum, col_sum = lax.psum((input_part, jnp.sum(squares, axis=0)), 'cls')  138 us
    reduce_scatter x1, waiting for transfers between devices, on_device(): lax.psum_scatter(partial_value, 'feat', scatter_dimension=0, tiled=True)  98.9 us
    pmax x1, blocking collectives, on_device(): row_top = lax.pmax(jnp.max(logits, axis=0), ('cls', 'feat'))  76.4 us
    all_gather x1, waiting for transfers between devices, on_device(): dlogits = lax.all_gather(own_dlogits, 'feat', axis=0, tiled=True)  51.6 us
    psum x1, blocking collectives, on_device(): row_sum = lax.psum(jnp.sum(squares, axis=1), 'feat')  21.3 us
  transfers between devices with their start and end apart: 2, of which 2 were waited for; matrix products, arithmetic and copies ran while one was open for 0% of the time, Pallas kernels for 0%

profile of v1, /device:TPU:1, one launch (start us, length us, event | category | flops | bytes accessed | tf_op | source)
XLA Modules:
  0.0 588.6 jit_solution(9742435272483267158)
XLA Ops:
  7.2 0.0 copy-start
  7.2 0.0 copy-start.5
  7.2 0.0 reduce-scatter.2.cloned.1.call-start
  7.2 1.0 copy-done
  8.2 7.8 %fusion.6 = f32[4096,512]{1,0:T(8,128)} fusion(bf16[4096,512]{1,0:T(8,128)(2,1)} %param.6, bf16[512,512]{1,0:T(8,128)(2,1)S(1)} %copy-done), kind=kOutput, calls=%fused_computation.17 | convolution fusion | flops 2147483648 | bytes 13107200 | tf_op jit(solution)/shard_map/dot_general | solution.py:23
  16.0 0.0 reduce-scatter.2.cloned.1.call-update
  16.0 0.0 all-gather.2.cloned.1.call-start
  16.1 98.9 %reduce-scatter.2.cloned.1.call-done = f32[512,512]{1,0:T(8,128)} async-done(((f32[4096,512]{1,0:T(8,128)}), f32[512,512]{1,0:T(8,128)}) %reduce-scatter.2.cloned.1.call-update) | async-done | bytes 1048592 | tf_op jit(solution)/shard_map/reduce_scatter | solution.py:26
  114.9 1.3 reduce_max.9
  116.3 76.4 %pmax.7 = f32[512]{0:T(512)S(1)} all-reduce(f32[512]{0:T(512)S(1)} %reduce_max.9), channel_id=1, replica_groups=mesh['cls'=32,'feat'=8] {'cls','feat'}, use_global_device_ids=true, to_apply=%region_2.3 | all-reduce | flops 512 | bytes 4096 | tf_op jit(solution)/shard_map/pmax | solution.py:30
  192.7 0.0 copy-done.5
  192.7 1.5 fusion.4
  194.2 72.3 %psum.42 = f32[512]{0:T(512)S(1)} all-reduce(f32[512]{0:T(512)S(1)} %get-tuple-element.8), channel_id=1, replica_groups=mesh['cls'=32,'feat'=8] {'cls','feat'}, use_global_device_ids=true, to_apply=%region_4.5 | all-reduce | flops 512 | bytes 4096 | tf_op jit(solution)/shard_map/psum | solution.py:32
  266.5 2.3 fusion.3
  268.8 0.0 all-gather.2.cloned.1.call-update
  268.8 51.6 %all-gather.2.cloned.1.call-done = bf16[4096,512]{1,0:T(8,128)(2,1)} async-done(((bf16[512,512]{1,0:T(8,128)(2,1)}), bf16[4096,512]{1,0:T(8,128)(2,1)}) %all-gather.2.cloned.1.call-update) | async-done | bytes 4194320 | tf_op jit(solution)/shard_map/all_gather | solution.py:35
  320.4 0.0 copy-start.1
  320.4 5.9 %fusion.7 = f32[512,512]{1,0:T(8,128)S(1)} fusion(bf16[4096,512]{1,0:T(8,128)(2,1)} %all-gather.2.cloned.1.call-done, bf16[4096,512]{1,0:T(8,128)(2,1)} %param.6), kind=kOutput, calls=%fused_computation.18 | convolution fusion | flops 2147483648 | bytes 9437184 | tf_op jit(solution)/shard_map/dot_general | solution.py:37
  326.4 0.0 copy-done.1
  326.4 0.0 copy-start.6
  326.4 0.0 copy-start.4
  326.4 6.0 %fusion.1 = (f32[4096]{0:T(1024)S(1)}, f32[512]{0:T(512)S(1)}, f32[4096,512]{1,0:T(8,128)}) fusion(bf16[4096,512]{1,0:T(8,128)(2,1)S(1)} %copy-done.1, bf16[512,512]{1,0:T(8,128)(2,1)S(1)} %copy-done), kind=kOutput, calls=%fused_computation.5 | convolution fusion | flops 2155867648 | bytes 13125632 | tf_op jit(solution)/shard_map/dot_general | solution.py:40
  332.4 21.3 %psum.45 = f32[4096]{0:T(1024)S(1)} all-reduce(f32[4096]{0:T(1024)S(1)} %get-tuple-element.5), channel_id=1, replica_groups=mesh['cls'=32,'feat'=8] {'feat'}, use_global_device_ids=true, to_apply=%region_9.10 | all-reduce | flops 4096 | bytes 32768 | tf_op jit(solution)/shard_map/psum | solution.py:44
  353.6 137.9 %all-reduce.3 = (bf16[512,512]{1,0:T(8,128)(2,1)}, f32[512]{0:T(512)S(1)}) all-reduce(f32[512,512]{1,0:T(8,128)S(1)} %fusion.7, f32[512]{0:T(512)S(1)} %get-tuple-element.6), channel_id=1, replica_groups=mesh['cls'=32,'feat'=8] {'cls'}, use_global_device_ids=true, to_apply=%region_5.6 | all-reduce | flops 262656 | bytes 1576960 | tf_op jit(solution)/shard_map/psum | solution.py:42
  491.5 0.0 copy-done.6
  491.5 0.0 copy-done.4
  491.6 0.0 copy-start.3
  491.6 0.0 copy-start.2
  491.6 5.6 multiply_reduce_fusion
  497.2 76.3 %all-reduce = (f32[512]{0:T(512)S(1)}, f32[]{:T(128)}) all-reduce(f32[512]{0:T(512)S(1)} %get-tuple-element.7, f32[]{:T(128)} %multiply_reduce_fusion), channel_id=1, replica_groups=mesh['cls'=32,'feat'=8] {'cls','feat'}, use_global_device_ids=true, to_apply=%region_7.8 | all-reduce | flops 513 | bytes 4104 | tf_op jit(solution)/shard_map/psum | solution.py:32
  574.3 6.9 %subtract_convert_fusion = bf16[4096,512]{1,0:T(8,128)(2,1)} fusion(bf16[4096,512]{1,0:T(8,128)(2,1)} %param.6, f32[4096,512]{1,0:T(8,128)} %get-tuple-element.13, f32[]{:T(128)S(6)} %mul.81, f32[512]{0:T(512)S(1)} %multiply_add_fusion.2, f32[4096]{0:T(1024)S(1)} %multiply_add_fusion.1), kind=kLoop, calls=%fused_computation | loop fusion | flops 12582912 | bytes 16795652 | tf_op jit(solution)/shard_map/convert_element_type | solution.py:51
  581.2 0.0 copy-done.3
  581.2 0.0 copy-done.2
  581.2 0.6 dynamic_slice.3
  (4 shorter events, 0.0 us)
Async XLA Ops:
  7.2 1.0 copy-start
  7.2 185.5 %copy-start.5 = (s32[512]{0:T(512)S(1)}, s32[512]{0:T(512)}, u32[]{:S(2)}) copy-start(s32[512]{0:T(512)} %param.7) | copy-start | bytes 6148
  7.2 107.8 %reduce-scatter.2.cloned.1.call-start = ((), (), s32[]{:S(2)}) async-start(), calls=%async_computation.1 | async-start | bytes 9437184 | tf_op jit(solution)/shard_map/reduce_scatter | solution.py:26
  16.0 304.4 %all-gather.2.cloned.1.call-start = ((), (), s32[]{:S(2)}) async-start(), calls=%async_computation.2 | async-start | bytes 4718592 | tf_op jit(solution)/shard_map/all_gather | solution.py:35
  320.4 6.0 %copy-start.1 = (bf16[4096,512]{1,0:T(8,128)(2,1)S(1)}, bf16[4096,512]{1,0:T(8,128)(2,1)}, u32[]{:S(2)}) copy-start(bf16[4096,512]{1,0:T(8,128)(2,1)} %all-gather.2.cloned.1.call-done) | copy-start | bytes 12582916
  326.4 165.2 %copy-start.6 = (f32[512]{0:T(512)S(1)}, f32[512]{0:T(512)}, u32[]{:S(2)}) copy-start(f32[512]{0:T(512)} %param.9) | copy-start | bytes 6148
  326.4 165.2 %copy-start.4 = (f32[4096]{0:T(1024)S(1)}, f32[4096]{0:T(1024)}, u32[]{:S(2)}) copy-start(f32[4096]{0:T(1024)} %param.8) | copy-start | bytes 49156
  491.6 89.7 %copy-start.3 = (f32[512]{0:T(512)}, f32[512]{0:T(512)S(1)}, u32[]{:S(2)}) copy-start(f32[512]{0:T(512)S(1)} %multiply_add_fusion.2) | copy-start | bytes 6148
  491.6 89.6 %copy-start.2 = (f32[4096]{0:T(1024)}, f32[4096]{0:T(1024)S(1)}, u32[]{:S(2)}) copy-start(f32[4096]{0:T(1024)S(1)} %multiply_add_fusion.1) | copy-start | bytes 49156
Sparse Core Ops, SparseCore 0:
  16.1 98.7 reduce-scatter.1
  268.9 51.4 all-gather.1

commit v2 on v0

v2 whole, which is shorter than its diff:
```python
import functools

import jax
import jax.numpy as jnp
from jax import lax
from jax.experimental import pallas as pl
from jax.experimental.pallas import tpu as pltpu
from jax.sharding import PartitionSpec as P

MESH = pl.DeviceIdType.MESH
F32, BF16 = jnp.float32, jnp.bfloat16

TINY_SQUARE = 1e-30
DECAY = 0.4
STEP_SIZE = 0.1
CLIP_LIMIT = 0.1

GROUPS = 2
SUBS = 4


def kernel(
    sizes,
    h_ref, w_hbm, target_ref, rm_ref, cm_ref,
    ig_ref, loss_ref, nw_hbm, nrm_ref, ncm_ref,
    w, first, part, slot, logit, dl, grad, acc_in,
    stat_z, stat_c, rsum, rscale, csum, usum_z, usum_c, in_parts, in_out,
    w_sem, out_sem, rs_send, rs_recv, ag_send, ag_recv, st_send, st_recv, in_send, in_recv, mo_send, mo_recv,
):
    nz, nc, D, V = sizes
    z, cls = lax.axis_index("feat"), lax.axis_index("cls")
    chunk, width = w.shape[1], w.shape[2]
    rows = logit.shape[2]
    half = chunk // 2
    piece = half // SUBS
    quarter = chunk // 4

    def ring(i):
        return lax.rem(z + (i + 2 * nz), nz)

    up, down = {"feat": ring(1)}, {"feat": ring(-1)}
    side = (up, down)

    loads = [pltpu.make_async_copy(w_hbm.at[o], w.at[o], w_sem.at[o]) for o in range(nz)]
    for load in loads:
        load.start()

    barrier = pltpu.get_barrier_semaphore()

    def greet(axis, me, n):
        def body(j, c):
            pl.semaphore_signal(barrier, inc=1, device_id={axis: lax.rem(me + j, n)}, device_id_type=MESH)
            return c
        lax.fori_loop(1, n, body, 0)

    greet("feat", z, nz)
    greet("cls", cls, nc)
    pl.semaphore_wait(barrier, nz - 1 + nc - 1)
    for load in loads:
        load.wait()

    def spread(axis, me, n, src, dst, ssem, rsem):
        def body(j, c):
            pltpu.make_async_remote_copy(
                src, dst, ssem, rsem, device_id={axis: lax.rem(me + j, n)}, device_id_type=MESH
            ).start()
            return c
        lax.fori_loop(1, n, body, 0)

    def wait_bytes(ref, sem):
        pltpu.make_async_copy(ref, ref, sem).wait()

    def partial_logits(p, d, c):
        return lax.dot_general(
            w[c, half * d : half * (d + 1), :], h_ref[rows * p : rows * (p + 1), :],
            (((1,), (1,)), ((), ())), preferred_element_type=F32,
        )

    def rs_first(p):
        for d in range(2):
            c = ring(-1) if d == 0 else ring(1)
            first[p, d] = partial_logits(p, d, c).reshape(SUBS, piece, rows)
            for k in range(SUBS):
                pltpu.make_async_remote_copy(
                    first.at[p, d, k], slot.at[p, 0, d, k], rs_send.at[p, d], rs_recv.at[p, 0, d, k],
                    device_id=side[d], device_id_type=MESH,
                ).start()

    def rs_ticks(p, low, high):
        def tick(s, carry):
            for d in range(2):
                c = ring(-1 - s) if d == 0 else ring(1 + s)
                part[d] = partial_logits(p, d, c).reshape(SUBS, piece, rows)
            for k in range(SUBS):
                for d in range(2):
                    wait_bytes(slot.at[p, s - 1, d, k], rs_recv.at[p, s - 1, d, k])
                    slot[p, s - 1, d, k] = slot[p, s - 1, d, k] + part[d, k]
                    pltpu.make_async_remote_copy(
                        slot.at[p, s - 1, d, k], slot.at[p, s, d, k], rs_send.at[p, d], rs_recv.at[p, s, d, k],
                        device_id=side[d], device_id_type=MESH,
                    ).start()
            return carry
        lax.fori_loop(low, high, tick, 0)

    def rs_last(p):
        for d in range(2):
            part[d] = partial_logits(p, d, z).reshape(SUBS, piece, rows)
        for k in range(SUBS):
            for d in range(2):
                wait_bytes(slot.at[p, nz - 2, d, k], rs_recv.at[p, nz - 2, d, k])
                at = half * d + piece * k
                logit[p, at : at + piece, :] = slot[p, nz - 2, d, k] + part[d, k]

    def mask(p):
        classes = lax.broadcasted_iota(jnp.int32, (chunk, rows), 0) + (cls * (nz * chunk) + z * chunk)
        return classes == target_ref[:, rows * p : rows * (p + 1)]

    def pack(top, total, picked):
        row = lax.broadcasted_iota(jnp.int32, (8, rows), 0)
        return jnp.where(row == 0, top, jnp.where(row == 1, total, jnp.where(row == 2, picked, 0.0)))

    def combine(stats, n):
        top = stats[0][0:1]
        for j in range(1, n):
            top = jnp.maximum(top, stats[j][0:1])
        total, picked = jnp.zeros_like(top), jnp.zeros_like(top)
        for j in range(n):
            total = total + stats[j][1:2] * jnp.exp(stats[j][0:1] - top)
            picked = picked + stats[j][2:3]
        return top, total, picked

    def stats_local(p):
        values = logit[p]
        top = jnp.max(values, axis=0, keepdims=True)
        total = jnp.sum(jnp.exp(values - top), axis=0, keepdims=True)
        picked = jnp.sum(jnp.where(mask(p), values, 0.0), axis=0, keepdims=True)
        stat_z[p, z] = pack(top, total, picked)
        spread("feat", z, nz, stat_z.at[p, z], stat_z.at[p, z], st_send.at[p, 0], st_recv.at[p, 0])

    def stats_middle(p):
        wait_bytes(stat_z.at[p, pl.ds(0, nz - 1)], st_recv.at[p, 0])
        stat_c[p, cls] = pack(*combine([stat_z[p, j] for j in range(nz)], nz))
        spread("cls", cls, nc, stat_c.at[p, cls], stat_c.at[p, cls], st_send.at[p, 1], st_recv.at[p, 1])

    def stats_last(p):
        wait_bytes(stat_c.at[p, pl.ds(0, nc - 1)], st_recv.at[p, 1])
        top, total, picked = combine([stat_c[p, j] for j in range(nc)], nc)
        loss_ref[:, rows * p : rows * (p + 1)] = jnp.log(total) + top - picked
        soft = jnp.exp(logit[p] - top) / total - mask(p).astype(F32)
        dl[p, z] = soft.astype(BF16)

    def ag_copy(p, d, hop, k, c):
        part_of = dl.at[p, c, pl.ds(quarter * k, quarter)]
        return pltpu.make_async_remote_copy(
            part_of, part_of, ag_send.at[p], ag_recv.at[p, hop, d, k], device_id=side[d], device_id_type=MESH
        )

    def ag_first(p):
        for k in range(4):
            for d in range(2):
                ag_copy(p, d, 0, k, z).start()

    def ag_tick(p, t):
        for k in range(4):
            for d in range(2):
                c = ring(-t) if d == 0 else ring(t)
                if t < nz // 2 or (k < 2) == (d == 0):
                    ag_copy(p, d, t - 1, k, c).wait_recv()
                if t + 1 < nz // 2 or (t + 1 == nz // 2 and (k < 2) == (d == 0)):
                    ag_copy(p, d, t, k, c).start()

    def consume(p, c):
        for j in range(2):
            term = lax.dot_general(
                dl[p, c], w[c, :, (width // 2) * j : (width // 2) * (j + 1)],
                (((0,), (0,)), ((), ())), preferred_element_type=F32,
            )
            acc_in[p, j] = acc_in[p, j] + term

        def body(k, carry):
            at = pl.ds(pl.multiple_of(quarter * k, quarter), quarter)
            term = jnp.dot(dl[p, c, at, :], h_ref[rows * p : rows * (p + 1), :], preferred_element_type=F32)
            if p > 0:
                term = grad[c, at, :] + term
            grad[c, at, :] = term
            if p == GROUPS - 1:
                square = term * term + TINY_SQUARE
                column = square[0:8]
                for i in range(1, quarter // 8):
                    column = column + square[8 * i : 8 * (i + 1)]
                csum_acc = carry + column
                lanes = square[:, 0:128]
                for i in range(1, width // 128):
                    lanes = lanes + square[:, 128 * i : 128 * (i + 1)]
                rsum[z, pl.ds(4 * c + k, 1), :] = jnp.sum(lanes.T, axis=0, keepdims=True)
                return csum_acc
            return carry

        return lax.fori_loop(0, 4, body, jnp.zeros((8, width), F32))

    blocks = nc // 2
    high = rows // blocks

    def in_send_parts(p):
        def place(q):
            return acc_in.at[p, lax.rem(q, 2), pl.ds(pl.multiple_of((q // 2) * high, high), high), :]

        in_parts[p, cls] = place(cls)[...]

        def body(j, c):
            q = lax.rem(cls + j, nc)
            pltpu.make_async_remote_copy(
                place(q), in_parts.at[p, cls], in_send.at[p, 0], in_recv.at[p, 0],
                device_id={"cls": q}, device_id_type=MESH,
            ).start()
            return c
        lax.fori_loop(1, nc, body, 0)

    def in_sum(p):
        wait_bytes(in_parts.at[p, pl.ds(0, nc - 1)], in_recv.at[p, 0])
        total = in_parts[p, 0]
        for q in range(1, nc):
            total = total + in_parts[p, q]
        in_out[p, cls] = total.astype(BF16)
        spread("cls", cls, nc, in_out.at[p, cls], in_out.at[p, cls], in_send.at[p, 1], in_recv.at[p, 1])

    def in_store(p):
        wait_bytes(in_out.at[p, pl.ds(0, nc - 1)], in_recv.at[p, 1])
        for q in range(nc):
            at, j = rows * p + (q // 2) * high, q % 2
            ig_ref[at : at + high, (width // 2) * j : (width // 2) * (j + 1)] = in_out[p, q]

    acc_in[...] = jnp.zeros_like(acc_in)
    rs_first(0)
    rs_ticks(0, 1, nz - 1)
    rs_first(1)
    rs_last(0)
    stats_local(0)
    rs_ticks(1, 1, 2)
    stats_middle(0)
    rs_ticks(1, 2, 3)
    stats_last(0)
    rs_ticks(1, 3, nz - 1)
    ag_first(0)
    rs_last(1)
    stats_local(1)
    consume(0, z)
    ag_tick(0, 1)
    stats_middle(1)
    consume(0, ring(-1))
    consume(0, ring(1))
    ag_tick(0, 2)
    stats_last(1)
    ag_first(1)
    consume(0, ring(-2))
    consume(0, ring(2))
    ag_tick(0, 3)
    consume(0, ring(-3))
    consume(0, ring(3))
    ag_tick(0, 4)
    consume(0, ring(4))
    in_send_parts(0)
    column = consume(1, z)
    ag_tick(1, 1)
    column = column + consume(1, ring(-1))
    column = column + consume(1, ring(1))
    ag_tick(1, 2)
    in_sum(0)
    column = column + consume(1, ring(-2))
    column = column + consume(1, ring(2))
    ag_tick(1, 3)
    in_store(0)
    column = column + consume(1, ring(-3))
    column = column + consume(1, ring(3))
    ag_tick(1, 4)
    column = column + consume(1, ring(4))

    spread("feat", z, nz, rsum.at[z], rsum.at[z], mo_send.at[0], mo_recv.at[0])
    column = jnp.sum(column, axis=0, keepdims=True)
    for i in range(width // 128):
        csum[cls, i : i + 1, :] = column[:, 128 * i : 128 * (i + 1)]
    spread("cls", cls, nc, csum.at[cls], csum.at[cls], mo_send.at[1], mo_recv.at[1])
    in_send_parts(1)

    wait_bytes(rsum.at[pl.ds(0, nz - 1)], mo_recv.at[0])
    row_sum = rsum[0]
    for j in range(1, nz):
        row_sum = row_sum + rsum[j]
    new_rm = DECAY * rm_ref[...] + (1.0 - DECAY) * (row_sum / D)
    nrm_ref[...] = new_rm
    rscale[...] = lax.rsqrt(new_rm)
    wait_bytes(csum.at[pl.ds(0, nc - 1)], mo_recv.at[1])
    col_sum = csum[0]
    for j in range(1, nc):
        col_sum = col_sum + csum[j]
    for i in range(width // 128):
        ncm_ref[:, 128 * i : 128 * (i + 1)] = (
            DECAY * cm_ref[:, 128 * i : 128 * (i + 1)] + (1.0 - DECAY) * (col_sum[i : i + 1] / V)
        )
    col_scale = lax.rsqrt(ncm_ref[...])

    def scale(i, carry):
        c, k = i // 4, lax.rem(i, 4)
        at = pl.ds(pl.multiple_of(quarter * k, quarter), quarter)
        row_scale = jnp.broadcast_to(rscale[pl.ds(i, 1), :], (128, 128)).T
        for j in range(width // 128):
            lanes = slice(128 * j, 128 * (j + 1))
            update = grad[c, at, lanes] * row_scale * col_scale[:, lanes]
            grad[c, at, lanes] = update
            square = update * update
            for r in range(quarter // 8):
                carry = carry + square[8 * r : 8 * (r + 1)]
        return carry

    usum_z[z] = lax.fori_loop(0, 4 * nz, scale, jnp.zeros((8, 128), F32))
    spread("feat", z, nz, usum_z.at[z], usum_z.at[z], mo_send.at[2], mo_recv.at[2])
    in_sum(1)
    wait_bytes(usum_z.at[pl.ds(0, nz - 1)], mo_recv.at[2])
    total = usum_z[0]
    for j in range(1, nz):
        total = total + usum_z[j]
    usum_c[cls] = total
    spread("cls", cls, nc, usum_c.at[cls], usum_c.at[cls], mo_send.at[3], mo_recv.at[3])
    wait_bytes(usum_c.at[pl.ds(0, nc - 1)], mo_recv.at[3])
    total = usum_c[0]
    for j in range(1, nc):
        total = total + usum_c[j]
    update_square = jnp.sum(total, keepdims=True)
    update_rms = jnp.sqrt(update_square / (V * D))
    factor = STEP_SIZE * (1.0 / jnp.maximum(1.0, update_rms / CLIP_LIMIT))

    for o in range(nz):
        def write(k, carry, o=o):
            at = pl.ds(pl.multiple_of(quarter * k, quarter), quarter)
            w[o, at, :] = (w[o, at, :].astype(F32) - factor * grad[o, at, :]).astype(BF16)
            return carry
        lax.fori_loop(0, 4, write, 0)
        pltpu.make_async_copy(w.at[o], nw_hbm.at[o], out_sem.at[o]).start()
    in_store(1)

    for o in range(nz):
        pltpu.make_async_copy(w.at[o], nw_hbm.at[o], out_sem.at[o]).wait()
    for p in range(GROUPS):
        for d in range(2):
            wait_bytes(slot.at[p, :, d], rs_send.at[p, d])
        wait_bytes(dl.at[p, pl.ds(0, nz - 1)], ag_send.at[p])
        wait_bytes(stat_z.at[p, pl.ds(0, nz - 1)], st_send.at[p, 0])
        wait_bytes(stat_c.at[p, pl.ds(0, nc - 1)], st_send.at[p, 1])
        wait_bytes(in_parts.at[p, pl.ds(0, nc - 1)], in_send.at[p, 0])
        wait_bytes(in_out.at[p, pl.ds(0, nc - 1)], in_send.at[p, 1])
    wait_bytes(rsum.at[pl.ds(0, nz - 1)], mo_send.at[0])
    wait_bytes(csum.at[pl.ds(0, nc - 1)], mo_send.at[1])
    wait_bytes(usum_z.at[pl.ds(0, nz - 1)], mo_send.at[2])
    wait_bytes(usum_c.at[pl.ds(0, nc - 1)], mo_send.at[3])


def solution(mesh):
    nz, nc = mesh.shape["feat"], mesh.shape["cls"]

    def on_device(hidden, weight, target, row_moment, col_moment):
        all_rows, width = hidden.shape
        classes = weight.shape[0]
        rows, chunk = all_rows // GROUPS, classes // nz
        piece = chunk // 2 // SUBS
        sizes = (nz, nc, width * nz, classes * nc)
        vmem = pl.BlockSpec(memory_space=pltpu.VMEM)
        hbm = pl.BlockSpec(memory_space=pl.ANY)
        dma = pltpu.SemaphoreType.DMA
        high = rows // (nc // 2)
        input_grad, loss, new_weight, nrm, ncm = pl.pallas_call(
            functools.partial(kernel, sizes),
            out_shape=(
                jax.ShapeDtypeStruct((all_rows, width), BF16),
                jax.ShapeDtypeStruct((1, all_rows), F32),
                jax.ShapeDtypeStruct((nz, chunk, width), BF16),
                jax.ShapeDtypeStruct((classes // 128, 128), F32),
                jax.ShapeDtypeStruct((1, width), F32),
            ),
            in_specs=[vmem, hbm, vmem, vmem, vmem],
            out_specs=(vmem, vmem, hbm, vmem, vmem),
            scratch_shapes=[
                pltpu.VMEM((nz, chunk, width), BF16),
                pltpu.VMEM((GROUPS, 2, SUBS, piece, rows), F32),
                pltpu.VMEM((2, SUBS, piece, rows), F32),
                pltpu.VMEM((GROUPS, nz - 1, 2, SUBS, piece, rows), F32),
                pltpu.VMEM((GROUPS, chunk, rows), F32),
                pltpu.VMEM((GROUPS, nz, chunk, rows), BF16),
                pltpu.VMEM((nz, chunk, width), F32),
                pltpu.VMEM((GROUPS, 2, rows, width // 2), F32),
                pltpu.VMEM((GROUPS, nz, 8, rows), F32),
                pltpu.VMEM((GROUPS, nc, 8, rows), F32),
                pltpu.VMEM((nz, classes // 128, 128), F32),
                pltpu.VMEM((classes // 128, 128), F32),
                pltpu.VMEM((nc, 8, 128), F32),
                pltpu.VMEM((nz, 8, 128), F32),
                pltpu.VMEM((nc, 8, 128), F32),
                pltpu.VMEM((GROUPS, nc, high, width // 2), F32),
                pltpu.VMEM((GROUPS, nc, high, width // 2), BF16),
                dma((nz,)),
                dma((nz,)),
                dma((GROUPS, 2)),
                dma((GROUPS, nz - 1, 2, SUBS)),
                dma((GROUPS,)),
                dma((GROUPS, nz // 2, 2, 4)),
                dma((GROUPS, 2)),
                dma((GROUPS, 2)),
                dma((GROUPS, 2)),
                dma((GROUPS, 2)),
                dma((4,)),
                dma((4,)),
            ],
            compiler_params=pltpu.CompilerParams(
                collective_id=0, has_side_effects=True, vmem_limit_bytes=56 * 2**20
            ),
            cost_estimate=pl.CostEstimate(
                flops=6 * all_rows * classes * width, bytes_accessed=4 * classes * width, transcendentals=0
            ),
        )(
            hidden, weight.reshape(nz, chunk, width), target.reshape(1, all_rows),
            row_moment.reshape(classes // 128, 128), col_moment.reshape(1, width),
        )
        share = all_rows // nz
        own_loss = lax.dynamic_slice_in_dim(loss.reshape(all_rows), lax.axis_index("feat") * share, share, 0)
        return input_grad, own_loss, new_weight.reshape(classes, width), nrm.reshape(classes), ncm.reshape(width)

    return jax.shard_map(
        on_device,
        mesh=mesh,
        in_specs=(P(None, "feat"), P("cls", "feat"), P(), P("cls"), P("feat")),
        out_specs=(P(None, "feat"), P("feat"), P("cls", "feat"), P("cls"), P("feat")),
        check_vma=False,
    )
```

time: 617 us -> 181 us (0.29)
  blocking collectives: 365 us -> 0 us
  waiting for transfers between devices: 192 us -> 0 us
  Pallas kernels: 0 us -> 171 us
  other arithmetic: 26.2 us -> 0 us
  matrix products: 16.1 us -> 0 us
  between operations: 14.8 us -> 0.65 us
  local copies, waits for them, and re-layouts: 1.61 us -> 8.79 us
    psum x4 -> x0, blocking collectives: 303 us -> none  [the longest x1 138 us: on_device(): input_sum, col_sum = lax.psum((input_part, jnp.sum(squares, axis=0)), 'cls')]
    psum x1 -> x0, waiting for transfers between devices: 192 us -> none  [on_device(): logits = lax.psum(partial_value, 'feat')]
    pallas_call x0 -> x1, Pallas kernels: none -> 171 us  [on_device(): pl.pallas_call(functools.partial(kernel, sizes), out_shape=(jax.ShapeDtyp...]
    pmax x1 -> x0, blocking collectives: 62.7 us -> none  [on_device(): row_top = lax.pmax(jnp.max(logits, axis=1), 'cls')]
    dot_general x3 -> x0, matrix products: 16.1 us -> none  [the longest x1 7.77 us: on_device(): lax.dot_general(hidden_states, weight, contract_feat, preferred_element_t...]
    convert_element_type x2 -> x0, other arithmetic: 12 us -> none  [the longest x1 6.92 us: on_device(): (weight.astype(jnp.float32) - step_size * clip_scale * update).astype(jnp...]
    reduce_sum x2 -> x0, other arithmetic: 10.3 us -> none  [the longest x1 5.59 us: on_device(): update_square = lax.psum(jnp.sum(update * update), ('cls', 'feat'))]
    unnamed x14 -> x8, local copies, waits for them, and re-layouts: 1.02 us -> 7.54 us
  transfers between devices with their start and end apart: 1 -> 0, of which waited for: 1 -> 0; matrix products, arithmetic and copies ran while one was open for 0% -> 0% of each run, Pallas kernels for 0% -> 0%
where the time goes in v2:
time: 181 us
  Pallas kernels  171 us (94%)
  local copies, waits for them, and re-layouts  8.79 us (5%)
    pallas_call x1, Pallas kernels, on_device(): pl.pallas_call(functools.partial(kernel, sizes), out_shape=(jax.ShapeDtyp...  171 us
    unnamed x8, local copies, waits for them, and re-layouts  7.54 us

profile of v2, /device:TPU:1, one launch (start us, length us, event | category | flops | bytes accessed | tf_op | source)
XLA Modules:
  0.0 180.7 jit_solution(4282234371888096040)
XLA Ops:
  0.6 171.3 %shard_map.92 = (bf16[512,512]{1,0:T(8,128)(2,1)}, f32[1,512]{1,0:T(1,128)}, bf16[8,512,512]{2,1,0:T(8,128)(2,1)}, f32[32,128]{1,0:T(8,128)}, f32[1,512]{1,0:T(1,128)}) custom-call(bf16[512,512]{1,0:T(8,128)(2,1)} %h_ref.1, bf16[8,512,512]{2,1,0:T(8,128)(2,1)} %bitcast.12, s32[1,512]{1,0:T(1,128)} %bitcast.14, f32[32,128]{1,0:T(8,128)} %bitcast.13, ...), custom_call_target="tpu_custom_call" | custom-call | flops 6442450944 | bytes 8388608 | tf_op jit(solution)/shard_map/pallas_call | solution.py:370
  171.9 1.2 dynamic-slice_bitcast_fusion
  173.2 1.9 %copy.14 = bf16[512,512]{1,0:T(8,128)(2,1)} copy(bf16[512,512]{1,0:T(8,128)(2,1)} %get-tuple-element.20) | data formatting | bytes 1048576
  175.0 0.0 copy-start
  175.0 0.0 copy-start.1
  175.1 4.5 %copy.15 = bf16[4096,512]{1,0:T(8,128)(2,1)} copy(bf16[4096,512]{1,0:T(8,128)(2,1)} %bitcast.9) | data formatting | bytes 8388608
  179.5 0.0 copy-done
  179.5 0.6 copy.16
  180.1 0.0 copy-done.1
  180.1 0.6 copy.17
Async XLA Ops:
  175.0 4.5 %copy-start = (f32[32,128]{1,0:T(8,128)S(1)}, f32[32,128]{1,0:T(8,128)}, u32[]{:S(2)}) copy-start(f32[32,128]{1,0:T(8,128)} %get-tuple-element.13) | copy-start | bytes 49156
  175.0 5.1 %copy-start.1 = (f32[1,512]{1,0:T(1,128)S(1)}, f32[1,512]{1,0:T(1,128)}, u32[]{:S(2)}) copy-start(f32[1,512]{1,0:T(1,128)} %get-tuple-element.14) | copy-start | bytes 6148

commit v3 on v2

--- a/solution.py
+++ b/solution.py
@@ -17,15 +17,18 @@
 
 GROUPS = 2
 SUBS = 4
+LOW = 8
+PER = 16 // LOW
+MOST = 2.0 ** (15 + LOW) - 16.0
 
 
 def kernel(
     sizes,
     h_ref, w_hbm, target_ref, rm_ref, cm_ref,
     ig_ref, loss_ref, nw_hbm, nrm_ref, ncm_ref,
-    w, first, part, slot, logit, dl, grad, acc_in,
+    w, first, part, slot, bound, logit, dl, grad, acc_in,
     stat_z, stat_c, rsum, rscale, csum, usum_z, usum_c, in_parts, in_out,
-    w_sem, out_sem, rs_send, rs_recv, ag_send, ag_recv, st_send, st_recv, in_send, in_recv, mo_send, mo_recv,
+    w_sem, out_sem, rs_send, rs_recv, bd_send, bd_recv, ag_send, ag_recv, st_send, st_recv, in_send, in_recv, mo_send, mo_recv,
 ):
     nz, nc, D, V = sizes
     z, cls = lax.axis_index("feat"), lax.axis_index("cls")
@@ -76,11 +79,40 @@
             (((1,), (1,)), ((), ())), preferred_element_type=F32,
         )
 
+    def encode(ref, value, top):
+        number = jnp.round(value * (MOST / top)).astype(jnp.int32)
+        ref[0:piece, :] = (number >> LOW).astype(jnp.int16)
+        low = number & (2**LOW - 1)
+        step = piece // PER
+        word = low[0:step]
+        for i in range(1, PER):
+            word = word + (low[step * i : step * (i + 1)] << (LOW * i))
+        ref[piece : piece + step, :] = (word - 32768).astype(jnp.int16)
+
+    def decode(ref, top):
+        high = ref[0:piece, :].astype(jnp.int32) << LOW
+        word = ref[piece : piece + piece // PER, :].astype(jnp.int32) + 32768
+        low = [(word >> (LOW * i)) & (2**LOW - 1) for i in range(PER)]
+        return (high + jnp.concatenate(low, axis=0)).astype(F32) * (top * (1.0 / MOST))
+
+    def largest(value):
+        return jnp.max(jnp.abs(value), axis=0, keepdims=True)
+
+    def bound_copy(p, s, d):
+        return pltpu.make_async_remote_copy(
+            bound.at[p, d, s, pl.ds(0, 1)], bound.at[p, d, s + 1, pl.ds(0, 1)], bd_send.at[p, d], bd_recv.at[p, s, d],
+            device_id=side[d], device_id_type=MESH,
+        )
+
     def rs_first(p):
         for d in range(2):
             c = ring(-1) if d == 0 else ring(1)
-            first[p, d] = partial_logits(p, d, c).reshape(SUBS, piece, rows)
+            value = partial_logits(p, d, c)
+            top = jnp.maximum(largest(value), 1e-30)
+            bound[p, d, 0, 0:1] = top
+            bound_copy(p, 0, d).start()
             for k in range(SUBS):
+                encode(first.at[p, d, k], value[piece * k : piece * (k + 1)], top)
                 pltpu.make_async_remote_copy(
                     first.at[p, d, k], slot.at[p, 0, d, k], rs_send.at[p, d], rs_recv.at[p, 0, d, k],
                     device_id=side[d], device_id_type=MESH,
@@ -88,15 +120,23 @@
 
     def rs_ticks(p, low, high):
         def tick(s, carry):
+            was, top = [], []
             for d in range(2):
                 c = ring(-1 - s) if d == 0 else ring(1 + s)
-                part[d] = partial_logits(p, d, c).reshape(SUBS, piece, rows)
+                value = partial_logits(p, d, c)
+                part[d] = value.reshape(SUBS, piece, rows)
+                bound_copy(p, s - 1, d).wait_recv()
+                was.append(bound[p, d, s, 0:1])
+                top.append(was[d] + largest(value))
+                bound[p, d, s, 0:1] = top[d]
+                bound_copy(p, s, d).start()
             for k in range(SUBS):
                 for d in range(2):
-                    wait_bytes(slot.at[p, s - 1, d, k], rs_recv.at[p, s - 1, d, k])
-                    slot[p, s - 1, d, k] = slot[p, s - 1, d, k] + part[d, k]
+                    here = slot.at[p, s - 1, d, k]
+                    wait_bytes(here, rs_recv.at[p, s - 1, d, k])
+                    encode(here, decode(here, was[d]) + part[d, k], top[d])
                     pltpu.make_async_remote_copy(
-                        slot.at[p, s - 1, d, k], slot.at[p, s, d, k], rs_send.at[p, d], rs_recv.at[p, s, d, k],
+                        here, slot.at[p, s, d, k], rs_send.at[p, d], rs_recv.at[p, s, d, k],
                         device_id=side[d], device_id_type=MESH,
                     ).start()
             return carry
@@ -105,11 +145,12 @@
     def rs_last(p):
         for d in range(2):
             part[d] = partial_logits(p, d, z).reshape(SUBS, piece, rows)
+            bound_copy(p, nz - 2, d).wait_recv()
         for k in range(SUBS):
             for d in range(2):
                 wait_bytes(slot.at[p, nz - 2, d, k], rs_recv.at[p, nz - 2, d, k])
                 at = half * d + piece * k
-                logit[p, at : at + piece, :] = slot[p, nz - 2, d, k] + part[d, k]
+                logit[p, at : at + piece, :] = decode(slot.at[p, nz - 2, d, k], bound[p, d, nz - 1, 0:1]) + part[d, k]
 
     def mask(p):
         classes = lax.broadcasted_iota(jnp.int32, (chunk, rows), 0) + (cls * (nz * chunk) + z * chunk)
@@ -343,6 +384,7 @@
     for p in range(GROUPS):
         for d in range(2):
             wait_bytes(slot.at[p, :, d], rs_send.at[p, d])
+            wait_bytes(bound.at[p, d, pl.ds(0, nz - 1), pl.ds(0, 1)], bd_send.at[p, d])
         wait_bytes(dl.at[p, pl.ds(0, nz - 1)], ag_send.at[p])
         wait_bytes(stat_z.at[p, pl.ds(0, nz - 1)], st_send.at[p, 0])
         wait_bytes(stat_c.at[p, pl.ds(0, nc - 1)], st_send.at[p, 1])
@@ -362,6 +404,7 @@
         classes = weight.shape[0]
         rows, chunk = all_rows // GROUPS, classes // nz
         piece = chunk // 2 // SUBS
+        words = piece + piece // PER
         sizes = (nz, nc, width * nz, classes * nc)
         vmem = pl.BlockSpec(memory_space=pltpu.VMEM)
         hbm = pl.BlockSpec(memory_space=pl.ANY)
@@ -380,9 +423,10 @@
             out_specs=(vmem, vmem, hbm, vmem, vmem),
             scratch_shapes=[
                 pltpu.VMEM((nz, chunk, width), BF16),
-                pltpu.VMEM((GROUPS, 2, SUBS, piece, rows), F32),
+                pltpu.VMEM((GROUPS, 2, SUBS, words, rows), jnp.int16),
                 pltpu.VMEM((2, SUBS, piece, rows), F32),
-                pltpu.VMEM((GROUPS, nz - 1, 2, SUBS, piece, rows), F32),
+                pltpu.VMEM((GROUPS, nz - 1, 2, SUBS, words, rows), jnp.int16),
+                pltpu.VMEM((GROUPS, 2, nz, 8, rows), F32),
                 pltpu.VMEM((GROUPS, chunk, rows), F32),
                 pltpu.VMEM((GROUPS, nz, chunk, rows), BF16),
                 pltpu.VMEM((nz, chunk, width), F32),
@@ -400,6 +444,8 @@
                 dma((nz,)),
                 dma((GROUPS, 2)),
                 dma((GROUPS, nz - 1, 2, SUBS)),
+                dma((GROUPS, 2)),
+                dma((GROUPS, nz - 1, 2)),
                 dma((GROUPS,)),
                 dma((GROUPS, nz // 2, 2, 4)),
                 dma((GROUPS, 2)),

time: 181 us -> 164 us (0.906)
  Pallas kernels: 171 us -> 155 us
    pallas_call x1, Pallas kernels: 171 us -> 155 us  [on_device(): pl.pallas_call(functools.partial(kernel, sizes), out_shape=(jax.ShapeDtyp...]
where the time goes in v3:
time: 164 us
  Pallas kernels  155 us (95%)
  local copies, waits for them, and re-layouts  8.79 us (5%)
    pallas_call x1, Pallas kernels, on_device(): pl.pallas_call(functools.partial(kernel, sizes), out_shape=(jax.ShapeDtyp...  155 us
    unnamed x8, local copies, waits for them, and re-layouts  7.54 us

profile of v3, /device:TPU:1, one launch (start us, length us, event | category | flops | bytes accessed | tf_op | source)
XLA Modules:
  0.0 164.0 jit_solution(14289704154110263329)
XLA Ops:
  0.6 154.6 %shard_map.92 = (bf16[512,512]{1,0:T(8,128)(2,1)}, f32[1,512]{1,0:T(1,128)}, bf16[8,512,512]{2,1,0:T(8,128)(2,1)}, f32[32,128]{1,0:T(8,128)}, f32[1,512]{1,0:T(1,128)}) custom-call(bf16[512,512]{1,0:T(8,128)(2,1)} %h_ref.1, bf16[8,512,512]{2,1,0:T(8,128)(2,1)} %bitcast.12, s32[1,512]{1,0:T(1,128)} %bitcast.14, f32[32,128]{1,0:T(8,128)} %bitcast.13, ...), custom_call_target="tpu_custom_call" | custom-call | flops 6442450944 | bytes 8388608 | tf_op jit(solution)/shard_map/pallas_call | solution.py:413
  155.2 1.2 dynamic-slice_bitcast_fusion
  156.5 1.9 %copy.14 = bf16[512,512]{1,0:T(8,128)(2,1)} copy(bf16[512,512]{1,0:T(8,128)(2,1)} %get-tuple-element.20) | data formatting | bytes 1048576
  158.3 0.0 copy-start
  158.3 0.0 copy-start.1
  158.3 4.5 %copy.15 = bf16[4096,512]{1,0:T(8,128)(2,1)} copy(bf16[4096,512]{1,0:T(8,128)(2,1)} %bitcast.9) | data formatting | bytes 8388608
  162.8 0.0 copy-done
  162.8 0.6 copy.16
  163.4 0.0 copy-done.1
  163.4 0.6 copy.17
Async XLA Ops:
  158.3 4.5 %copy-start = (f32[32,128]{1,0:T(8,128)S(1)}, f32[32,128]{1,0:T(8,128)}, u32[]{:S(2)}) copy-start(f32[32,128]{1,0:T(8,128)} %get-tuple-element.13) | copy-start | bytes 49156
  158.3 5.1 %copy-start.1 = (f32[1,512]{1,0:T(1,128)S(1)}, f32[1,512]{1,0:T(1,128)}, u32[]{:S(2)}) copy-start(f32[1,512]{1,0:T(1,128)} %get-tuple-element.14) | copy-start | bytes 6148

commit v4 on v3

--- a/solution.py
+++ b/solution.py
@@ -24,11 +24,11 @@
 
 def kernel(
     sizes,
-    h_ref, w_hbm, target_ref, rm_ref, cm_ref,
-    ig_ref, loss_ref, nw_hbm, nrm_ref, ncm_ref,
-    w, first, part, slot, bound, logit, dl, grad, acc_in,
+    h_hbm, w_hbm, target_hbm, rm_hbm, cm_hbm,
+    w, grad, ig_ref, loss_ref, nrm_ref, ncm_ref, factor_ref,
+    h_ref, target_ref, rm_ref, cm_ref, first, part, slot, bound, logit, dl, acc_in,
     stat_z, stat_c, rsum, rscale, csum, usum_z, usum_c, in_parts, in_out,
-    w_sem, out_sem, rs_send, rs_recv, bd_send, bd_recv, ag_send, ag_recv, st_send, st_recv, in_send, in_recv, mo_send, mo_recv,
+    w_sem, rs_send, rs_recv, bd_send, bd_recv, ag_send, ag_recv, st_send, st_recv, in_send, in_recv, mo_send, mo_recv,
 ):
     nz, nc, D, V = sizes
     z, cls = lax.axis_index("feat"), lax.axis_index("cls")
@@ -44,7 +44,10 @@
     up, down = {"feat": ring(1)}, {"feat": ring(-1)}
     side = (up, down)
 
-    loads = [pltpu.make_async_copy(w_hbm.at[o], w.at[o], w_sem.at[o]) for o in range(nz)]
+    loads = [pltpu.make_async_copy(h_hbm, h_ref, w_sem.at[nz])]
+    loads += [pltpu.make_async_copy(w_hbm.at[o], w.at[o], w_sem.at[o]) for o in range(nz)]
+    small = ((target_hbm, target_ref), (rm_hbm, rm_ref), (cm_hbm, cm_ref))
+    loads += [pltpu.make_async_copy(a, b, w_sem.at[nz + 1 + i]) for i, (a, b) in enumerate(small)]
     for load in loads:
         load.start()
 
@@ -201,43 +204,49 @@
             for d in range(2):
                 ag_copy(p, d, 0, k, z).start()
 
-    def ag_tick(p, t):
-        for k in range(4):
-            for d in range(2):
-                c = ring(-t) if d == 0 else ring(t)
-                if t < nz // 2 or (k < 2) == (d == 0):
-                    ag_copy(p, d, t - 1, k, c).wait_recv()
-                if t + 1 < nz // 2 or (t + 1 == nz // 2 and (k < 2) == (d == 0)):
+    def ag_tick(p, t, column=None):
+        def take(d, k, column):
+            c = ring(-t) if d == 0 else ring(t)
+            ag_copy(p, d, t - 1, k, c).wait_recv()
+            if t + 1 < nz // 2:
+                ag_copy(p, d, t, k, c).start()
+            elif t + 1 == nz // 2:
+                @pl.when(k < 2 if d == 0 else k >= 2)
+                def _():
                     ag_copy(p, d, t, k, c).start()
-
-    def consume(p, c):
+            return consume(p, c, k, column)
+
+        def body(k, column):
+            return take(1, k + 2 if t == nz // 2 else k, take(0, k, column))
+
+        return lax.fori_loop(0, 2 if t == nz // 2 else 4, body, no_column if column is None else column)
+
+    no_column = jnp.zeros((8, width), F32)
+
+    def consume(p, c, k, column):
+        at = pl.ds(pl.multiple_of(quarter * k, quarter), quarter)
+        term = lax.dot_general(
+            dl[p, c, at, :], w[c, at, :], (((0,), (0,)), ((), ())), preferred_element_type=F32
+        )
         for j in range(2):
-            term = lax.dot_general(
-                dl[p, c], w[c, :, (width // 2) * j : (width // 2) * (j + 1)],
-                (((0,), (0,)), ((), ())), preferred_element_type=F32,
-            )
-            acc_in[p, j] = acc_in[p, j] + term
-
-        def body(k, carry):
-            at = pl.ds(pl.multiple_of(quarter * k, quarter), quarter)
-            term = jnp.dot(dl[p, c, at, :], h_ref[rows * p : rows * (p + 1), :], preferred_element_type=F32)
-            if p > 0:
-                term = grad[c, at, :] + term
-            grad[c, at, :] = term
-            if p == GROUPS - 1:
-                square = term * term + TINY_SQUARE
-                column = square[0:8]
-                for i in range(1, quarter // 8):
-                    column = column + square[8 * i : 8 * (i + 1)]
-                csum_acc = carry + column
-                lanes = square[:, 0:128]
-                for i in range(1, width // 128):
-                    lanes = lanes + square[:, 128 * i : 128 * (i + 1)]
-                rsum[z, pl.ds(4 * c + k, 1), :] = jnp.sum(lanes.T, axis=0, keepdims=True)
-                return csum_acc
-            return carry
-
-        return lax.fori_loop(0, 4, body, jnp.zeros((8, width), F32))
+            acc_in[p, j] = acc_in[p, j] + term[:, (width // 2) * j : (width // 2) * (j + 1)]
+        term = jnp.dot(dl[p, c, at, :], h_ref[rows * p : rows * (p + 1), :], preferred_element_type=F32)
+        if p > 0:
+            term = grad[c, at, :] + term
+        grad[c, at, :] = term
+        if p < GROUPS - 1:
+            return column
+        square = term * term + TINY_SQUARE
+        for i in range(quarter // 8):
+            column = column + square[8 * i : 8 * (i + 1)]
+        lanes = square[:, 0:128]
+        for i in range(1, width // 128):
+            lanes = lanes + square[:, 128 * i : 128 * (i + 1)]
+        rsum[z, pl.ds(4 * c + k, 1), :] = jnp.sum(lanes.T, axis=0, keepdims=True)
+        return column
+
+    def consume_own(p):
+        return lax.fori_loop(0, 4, lambda k, column: consume(p, z, k, column), no_column)
 
     blocks = nc // 2
     high = rows // blocks
@@ -285,36 +294,22 @@
     ag_first(0)
     rs_last(1)
     stats_local(1)
-    consume(0, z)
+    consume_own(0)
     ag_tick(0, 1)
     stats_middle(1)
-    consume(0, ring(-1))
-    consume(0, ring(1))
     ag_tick(0, 2)
     stats_last(1)
     ag_first(1)
-    consume(0, ring(-2))
-    consume(0, ring(2))
     ag_tick(0, 3)
-    consume(0, ring(-3))
-    consume(0, ring(3))
+    column = consume_own(1)
+    column = ag_tick(1, 1, column)
     ag_tick(0, 4)
-    consume(0, ring(4))
     in_send_parts(0)
-    column = consume(1, z)
-    ag_tick(1, 1)
-    column = column + consume(1, ring(-1))
-    column = column + consume(1, ring(1))
-    ag_tick(1, 2)
+    column = ag_tick(1, 2, column)
     in_sum(0)
-    column = column + consume(1, ring(-2))
-    column = column + consume(1, ring(2))
-    ag_tick(1, 3)
+    column = ag_tick(1, 3, column)
     in_store(0)
-    column = column + consume(1, ring(-3))
-    column = column + consume(1, ring(3))
-    ag_tick(1, 4)
-    column = column + consume(1, ring(4))
+    column = ag_tick(1, 4, column)
 
     spread("feat", z, nz, rsum.at[z], rsum.at[z], mo_send.at[0], mo_recv.at[0])
     column = jnp.sum(column, axis=0, keepdims=True)
@@ -349,11 +344,12 @@
             update = grad[c, at, lanes] * row_scale * col_scale[:, lanes]
             grad[c, at, lanes] = update
             square = update * update
-            for r in range(quarter // 8):
-                carry = carry + square[8 * r : 8 * (r + 1)]
+            for r in range(quarter // 32):
+                carry = carry + square[32 * r : 32 * (r + 1)]
         return carry
 
-    usum_z[z] = lax.fori_loop(0, 4 * nz, scale, jnp.zeros((8, 128), F32))
+    squares = lax.fori_loop(0, 4 * nz, scale, jnp.zeros((32, 128), F32), unroll=2)
+    usum_z[z] = squares[0:8] + squares[8:16] + (squares[16:24] + squares[24:32])
     spread("feat", z, nz, usum_z.at[z], usum_z.at[z], mo_send.at[2], mo_recv.at[2])
     in_sum(1)
     wait_bytes(usum_z.at[pl.ds(0, nz - 1)], mo_recv.at[2])
@@ -370,17 +366,9 @@
     update_rms = jnp.sqrt(update_square / (V * D))
     factor = STEP_SIZE * (1.0 / jnp.maximum(1.0, update_rms / CLIP_LIMIT))
 
-    for o in range(nz):
-        def write(k, carry, o=o):
-            at = pl.ds(pl.multiple_of(quarter * k, quarter), quarter)
-            w[o, at, :] = (w[o, at, :].astype(F32) - factor * grad[o, at, :]).astype(BF16)
-            return carry
-        lax.fori_loop(0, 4, write, 0)
-        pltpu.make_async_copy(w.at[o], nw_hbm.at[o], out_sem.at[o]).start()
+    factor_ref[...] = jnp.broadcast_to(factor, factor_ref.shape)
     in_store(1)
 
-    for o in range(nz):
-        pltpu.make_async_copy(w.at[o], nw_hbm.at[o], out_sem.at[o]).wait()
     for p in range(GROUPS):
         for d in range(2):
             wait_bytes(slot.at[p, :, d], rs_send.at[p, d])
@@ -396,6 +384,27 @@
     wait_bytes(usum_c.at[pl.ds(0, nc - 1)], mo_send.at[3])
 
 
+def finish(share, w, update, ig_in, loss_in, nrm_in, ncm_in, factor_ref, ig_ref, loss_ref, nw_hbm, nrm_ref, ncm_ref, new_w, out_sem):
+    nz, chunk, width = w.shape
+    factor = factor_ref[0:1, 0:1]
+    copies = [pltpu.make_async_copy(new_w.at[o], nw_hbm.at[o], out_sem.at[o]) for o in range(nz)]
+    for o in range(nz):
+        def write(k, carry, o=o):
+            at = pl.ds(pl.multiple_of(64 * k, 64), 64)
+            new_w[o, at, :] = (w[o, at, :].astype(F32) - factor * update[o, at, :]).astype(BF16)
+            return carry
+        lax.fori_loop(0, chunk // 64, write, 0)
+        copies[o].start()
+    ig_ref[...] = ig_in[...]
+    rows = loss_in.shape[1]
+    loss = jnp.broadcast_to(loss_in[...], (8, rows))
+    loss_ref[...] = pltpu.roll(loss, lax.rem(rows - share * lax.axis_index("feat"), rows), 1)[0:1, 0:share]
+    nrm_ref[...] = nrm_in[...]
+    ncm_ref[...] = ncm_in[...]
+    for copy in copies:
+        copy.wait()
+
+
 def solution(mesh):
     nz, nc = mesh.shape["feat"], mesh.shape["cls"]
 
@@ -410,26 +419,30 @@
         hbm = pl.BlockSpec(memory_space=pl.ANY)
         dma = pltpu.SemaphoreType.DMA
         high = rows // (nc // 2)
-        input_grad, loss, new_weight, nrm, ncm = pl.pallas_call(
+        between = pl.pallas_call(
             functools.partial(kernel, sizes),
             out_shape=(
-                jax.ShapeDtypeStruct((all_rows, width), BF16),
-                jax.ShapeDtypeStruct((1, all_rows), F32),
-                jax.ShapeDtypeStruct((nz, chunk, width), BF16),
-                jax.ShapeDtypeStruct((classes // 128, 128), F32),
-                jax.ShapeDtypeStruct((1, width), F32),
+                pltpu.VMEM((nz, chunk, width), BF16),
+                pltpu.VMEM((nz, chunk, width), F32),
+                pltpu.VMEM((all_rows, width), BF16),
+                pltpu.VMEM((1, all_rows), F32),
+                pltpu.VMEM((classes // 128, 128), F32),
+                pltpu.VMEM((1, width), F32),
+                pltpu.VMEM((8, 128), F32),
             ),
-            in_specs=[vmem, hbm, vmem, vmem, vmem],
-            out_specs=(vmem, vmem, hbm, vmem, vmem),
+            in_specs=[hbm] * 5,
+            out_specs=(vmem,) * 7,
             scratch_shapes=[
-                pltpu.VMEM((nz, chunk, width), BF16),
+                pltpu.VMEM((all_rows, width), BF16),
+                pltpu.VMEM((1, all_rows), jnp.int32),
+                pltpu.VMEM((classes // 128, 128), F32),
+                pltpu.VMEM((1, width), F32),
                 pltpu.VMEM((GROUPS, 2, SUBS, words, rows), jnp.int16),
                 pltpu.VMEM((2, SUBS, piece, rows), F32),
                 pltpu.VMEM((GROUPS, nz - 1, 2, SUBS, words, rows), jnp.int16),
                 pltpu.VMEM((GROUPS, 2, nz, 8, rows), F32),
                 pltpu.VMEM((GROUPS, chunk, rows), F32),
                 pltpu.VMEM((GROUPS, nz, chunk, rows), BF16),
-                pltpu.VMEM((nz, chunk, width), F32),
                 pltpu.VMEM((GROUPS, 2, rows, width // 2), F32),
                 pltpu.VMEM((GROUPS, nz, 8, rows), F32),
                 pltpu.VMEM((GROUPS, nc, 8, rows), F32),
@@ -440,8 +453,7 @@
                 pltpu.VMEM((nc, 8, 128), F32),
                 pltpu.VMEM((GROUPS, nc, high, width // 2), F32),
                 pltpu.VMEM((GROUPS, nc, high, width // 2), BF16),
-                dma((nz,)),
-                dma((nz,)),
+                dma((nz + 4,)),
                 dma((GROUPS, 2)),
                 dma((GROUPS, nz - 1, 2, SUBS)),
                 dma((GROUPS, 2)),
@@ -456,7 +468,7 @@
                 dma((4,)),
             ],
             compiler_params=pltpu.CompilerParams(
-                collective_id=0, has_side_effects=True, vmem_limit_bytes=56 * 2**20
+                collective_id=0, has_side_effects=True, vmem_limit_bytes=51 * 2**20
             ),
             cost_estimate=pl.CostEstimate(
                 flops=6 * all_rows * classes * width, bytes_accessed=4 * classes * width, transcendentals=0
@@ -466,8 +478,22 @@
             row_moment.reshape(classes // 128, 128), col_moment.reshape(1, width),
         )
         share = all_rows // nz
-        own_loss = lax.dynamic_slice_in_dim(loss.reshape(all_rows), lax.axis_index("feat") * share, share, 0)
-        return input_grad, own_loss, new_weight.reshape(classes, width), nrm.reshape(classes), ncm.reshape(width)
+        input_grad, loss, new_weight, nrm, ncm = pl.pallas_call(
+            functools.partial(finish, share),
+            out_shape=(
+                jax.ShapeDtypeStruct((all_rows, width), BF16),
+                jax.ShapeDtypeStruct((1, share), F32),
+                jax.ShapeDtypeStruct((nz, chunk, width), BF16),
+                jax.ShapeDtypeStruct((classes // 128, 128), F32),
+                jax.ShapeDtypeStruct((1, width), F32),
+            ),
+            in_specs=[vmem] * 7,
+            out_specs=(vmem, vmem, hbm, vmem, vmem),
+            scratch_shapes=[pltpu.VMEM((nz, chunk, width), BF16), dma((nz,))],
+            compiler_params=pltpu.CompilerParams(vmem_limit_bytes=36 * 2**20),
+            cost_estimate=pl.CostEstimate(flops=2 * classes * width, bytes_accessed=2 * classes * width, transcendentals=0),
+        )(*between)
+        return input_grad, loss.reshape(share), new_weight.reshape(classes, width), nrm.reshape(classes), ncm.reshape(width)
 
     return jax.shard_map(
         on_device,

time: 164 us -> 148 us (0.902)
  local copies, waits for them, and re-layouts: 8.79 us -> 0 us
  Pallas kernels: 155 us -> 147 us
    unnamed x8 -> x0, local copies, waits for them, and re-layouts: 7.54 us -> none
    pallas_call x1 -> x2, Pallas kernels: 155 us -> 147 us  [the longest x1 144 us: on_device(): pl.pallas_call(functools.partial(kernel, sizes), out_shape=(pltpu.VMEM((n...]
where the time goes in v4:
time: 148 us
  Pallas kernels  147 us (99%)
    pallas_call x1, Pallas kernels, on_device(): pl.pallas_call(functools.partial(kernel, sizes), out_shape=(pltpu.VMEM((n...  144 us
    pallas_call x1, Pallas kernels, on_device(): pl.pallas_call(functools.partial(finish, share), out_shape=(jax.ShapeDtyp...  3.28 us

profile of v4, /device:TPU:1, one launch (start us, length us, event | category | flops | bytes accessed | tf_op | source)
XLA Modules:
  0.0 147.8 jit_solution(2959648575058226283)
XLA Ops:
  0.6 143.9 %shard_map.92 = (bf16[8,512,512]{2,1,0:T(8,128)(2,1)S(1)}, f32[8,512,512]{2,1,0:T(8,128)S(1)}, bf16[512,512]{1,0:T(8,128)(2,1)S(1)}, f32[1,512]{1,0:T(1,128)S(1)...) custom-call(bf16[512,512]{1,0:T(8,128)(2,1)} %h_hbm.1, bf16[8,512,512]{2,1,0:T(8,128)(2,1)} %bitcast.8, ...), custom_call_target="tpu_custom_call" | custom-call | flops 6442450944 | bytes 8388608 | tf_op jit(solution)/shard_map/pallas_call | solution.py:422
  144.5 3.3 %shard_map.93 = (bf16[512,512]{1,0:T(8,128)(2,1)}, f32[1,64]{1,0:T(1,128)}, bf16[8,512,512]{2,1,0:T(8,128)(2,1)}, f32[32,128]{1,0:T(8,128)}, f32[1,512]{1,0:T(1,128)}) custom-call(bf16[8,512,512]{2,1,0:T(8,128)(2,1)S(1)} %get-tuple-element.17.w, f32[8,512,512]{2,1,0:T(8,128)S(1)} %get-tuple-element.18.update, bf16[512,512]{1,0:T(8,128)(2,1)S(1)} %get-tuple-element.19.ig_in, ...), custom_call_target="tpu_custom_call" | custom-call | flops 4194304 | bytes 4194304 | tf_op jit(solution)/shard_map/pallas_call | solution.py:481

commit v5 on v4

--- a/solution.py
+++ b/solution.py
@@ -17,7 +17,8 @@
 
 GROUPS = 2
 SUBS = 4
-LOW = 8
+LAG = 2
+LOW = 4
 PER = 16 // LOW
 MOST = 2.0 ** (15 + LOW) - 16.0
 
@@ -26,7 +27,7 @@
     sizes,
     h_hbm, w_hbm, target_hbm, rm_hbm, cm_hbm,
     w, grad, ig_ref, loss_ref, nrm_ref, ncm_ref, factor_ref,
-    h_ref, target_ref, rm_ref, cm_ref, first, part, slot, bound, logit, dl, acc_in,
+    h_ref, target_ref, rm_ref, cm_ref, first, part, slot, bound, came, logit, dl, acc_in,
     stat_z, stat_c, rsum, rscale, csum, usum_z, usum_c, in_parts, in_out,
     w_sem, rs_send, rs_recv, bd_send, bd_recv, ag_send, ag_recv, st_send, st_recv, in_send, in_recv, mo_send, mo_recv,
 ):
@@ -82,15 +83,14 @@
             (((1,), (1,)), ((), ())), preferred_element_type=F32,
         )
 
-    def encode(ref, value, top):
+    def encode(value, top):
         number = jnp.round(value * (MOST / top)).astype(jnp.int32)
-        ref[0:piece, :] = (number >> LOW).astype(jnp.int16)
         low = number & (2**LOW - 1)
         step = piece // PER
-        word = low[0:step]
+        word = low[0:step] - 32768
         for i in range(1, PER):
             word = word + (low[step * i : step * (i + 1)] << (LOW * i))
-        ref[piece : piece + step, :] = (word - 32768).astype(jnp.int16)
+        return (number >> LOW).astype(jnp.int16), word.astype(jnp.int16)
 
     def decode(ref, top):
         high = ref[0:piece, :].astype(jnp.int32) << LOW
@@ -98,62 +98,58 @@
         low = [(word >> (LOW * i)) & (2**LOW - 1) for i in range(PER)]
         return (high + jnp.concatenate(low, axis=0)).astype(F32) * (top * (1.0 / MOST))
 
-    def largest(value):
-        return jnp.max(jnp.abs(value), axis=0, keepdims=True)
-
-    def bound_copy(p, s, d):
-        return pltpu.make_async_remote_copy(
-            bound.at[p, d, s, pl.ds(0, 1)], bound.at[p, d, s + 1, pl.ds(0, 1)], bd_send.at[p, d], bd_recv.at[p, s, d],
-            device_id=side[d], device_id_type=MESH,
-        )
+    def ring_send(p, s, k, refs, values):
+        tops = [jnp.maximum(jnp.max(jnp.abs(value), axis=0, keepdims=True), 1e-30) for value in values]
+        codes = [encode(value, top) for value, top in zip(values, tops)]
+        for d in range(2):
+            bound[p, d, s, pl.ds(k, 1)] = tops[d]
+            refs[d][0:piece, :] = codes[d][0]
+            refs[d][piece : piece + piece // PER, :] = codes[d][1]
+        for d in range(2):
+            pltpu.make_async_remote_copy(
+                bound.at[p, d, s, pl.ds(k, 1)], came.at[p, d, s, pl.ds(k, 1)], bd_send.at[p, d], bd_recv.at[p, s, d, k],
+                device_id=side[d], device_id_type=MESH,
+            ).start()
+            pltpu.make_async_remote_copy(
+                refs[d], slot.at[p, s, d, k], rs_send.at[p, d], rs_recv.at[p, s, d, k],
+                device_id=side[d], device_id_type=MESH,
+            ).start()
+
+    def ring_take(p, s, k):
+        for d in range(2):
+            wait_bytes(came.at[p, d, s, pl.ds(k, 1)], bd_recv.at[p, s, d, k])
+            wait_bytes(slot.at[p, s, d, k], rs_recv.at[p, s, d, k])
+        return [decode(slot.at[p, s, d, k], came[p, d, s, pl.ds(k, 1)]) + part[p, d, k] for d in range(2)]
 
     def rs_first(p):
+        value = [partial_logits(p, d, ring(-1) if d == 0 else ring(1)) for d in range(2)]
+        for k in range(SUBS):
+            ring_send(p, 0, k, [first.at[p, d, k] for d in range(2)], [value[d][piece * k : piece * (k + 1)] for d in range(2)])
+
+    def rs_tick(p, s):
         for d in range(2):
-            c = ring(-1) if d == 0 else ring(1)
-            value = partial_logits(p, d, c)
-            top = jnp.maximum(largest(value), 1e-30)
-            bound[p, d, 0, 0:1] = top
-            bound_copy(p, 0, d).start()
-            for k in range(SUBS):
-                encode(first.at[p, d, k], value[piece * k : piece * (k + 1)], top)
-                pltpu.make_async_remote_copy(
-                    first.at[p, d, k], slot.at[p, 0, d, k], rs_send.at[p, d], rs_recv.at[p, 0, d, k],
-                    device_id=side[d], device_id_type=MESH,
-                ).start()
+            c = ring(-1 - s) if d == 0 else ring(1 + s)
+            part[p, d] = partial_logits(p, d, c).reshape(SUBS, piece, rows)
+        for k in range(SUBS):
+            ring_send(p, s, k, [slot.at[p, s - 1, d, k] for d in range(2)], ring_take(p, s - 1, k))
 
     def rs_ticks(p, low, high):
+        lax.fori_loop(low, high, lambda s, carry: (rs_tick(p, s), carry)[1], 0)
+
+    def rs_both(low, high, lag):
         def tick(s, carry):
-            was, top = [], []
-            for d in range(2):
-                c = ring(-1 - s) if d == 0 else ring(1 + s)
-                value = partial_logits(p, d, c)
-                part[d] = value.reshape(SUBS, piece, rows)
-                bound_copy(p, s - 1, d).wait_recv()
-                was.append(bound[p, d, s, 0:1])
-                top.append(was[d] + largest(value))
-                bound[p, d, s, 0:1] = top[d]
-                bound_copy(p, s, d).start()
-            for k in range(SUBS):
-                for d in range(2):
-                    here = slot.at[p, s - 1, d, k]
-                    wait_bytes(here, rs_recv.at[p, s - 1, d, k])
-                    encode(here, decode(here, was[d]) + part[d, k], top[d])
-                    pltpu.make_async_remote_copy(
-                        here, slot.at[p, s, d, k], rs_send.at[p, d], rs_recv.at[p, s, d, k],
-                        device_id=side[d], device_id_type=MESH,
-                    ).start()
+            rs_tick(0, s)
+            rs_tick(1, s - lag)
             return carry
         lax.fori_loop(low, high, tick, 0)
 
     def rs_last(p):
         for d in range(2):
-            part[d] = partial_logits(p, d, z).reshape(SUBS, piece, rows)
-            bound_copy(p, nz - 2, d).wait_recv()
+            part[p, d] = partial_logits(p, d, z).reshape(SUBS, piece, rows)
         for k in range(SUBS):
-            for d in range(2):
-                wait_bytes(slot.at[p, nz - 2, d, k], rs_recv.at[p, nz - 2, d, k])
+            for d, value in enumerate(ring_take(p, nz - 2, k)):
                 at = half * d + piece * k
-                logit[p, at : at + piece, :] = decode(slot.at[p, nz - 2, d, k], bound[p, d, nz - 1, 0:1]) + part[d, k]
+                logit[p, at : at + piece, :] = value
 
     def mask(p):
         classes = lax.broadcasted_iota(jnp.int32, (chunk, rows), 0) + (cls * (nz * chunk) + z * chunk)
@@ -282,16 +278,17 @@
 
     acc_in[...] = jnp.zeros_like(acc_in)
     rs_first(0)
-    rs_ticks(0, 1, nz - 1)
+    rs_ticks(0, 1, LAG + 1)
     rs_first(1)
+    rs_both(LAG + 1, nz - 1, LAG)
     rs_last(0)
     stats_local(0)
-    rs_ticks(1, 1, 2)
+    rs_ticks(1, nz - 1 - LAG, nz - LAG)
     stats_middle(0)
-    rs_ticks(1, 2, 3)
+    rs_ticks(1, nz - LAG, nz + 1 - LAG)
     stats_last(0)
-    rs_ticks(1, 3, nz - 1)
     ag_first(0)
+    rs_ticks(1, nz + 1 - LAG, nz - 1)
     rs_last(1)
     stats_local(1)
     consume_own(0)
@@ -372,7 +369,7 @@
     for p in range(GROUPS):
         for d in range(2):
             wait_bytes(slot.at[p, :, d], rs_send.at[p, d])
-            wait_bytes(bound.at[p, d, pl.ds(0, nz - 1), pl.ds(0, 1)], bd_send.at[p, d])
+            wait_bytes(bound.at[p, d, pl.ds(0, nz - 1), pl.ds(0, SUBS)], bd_send.at[p, d])
         wait_bytes(dl.at[p, pl.ds(0, nz - 1)], ag_send.at[p])
         wait_bytes(stat_z.at[p, pl.ds(0, nz - 1)], st_send.at[p, 0])
         wait_bytes(stat_c.at[p, pl.ds(0, nc - 1)], st_send.at[p, 1])
@@ -438,9 +435,10 @@
                 pltpu.VMEM((classes // 128, 128), F32),
                 pltpu.VMEM((1, width), F32),
                 pltpu.VMEM((GROUPS, 2, SUBS, words, rows), jnp.int16),
-                pltpu.VMEM((2, SUBS, piece, rows), F32),
+                pltpu.VMEM((GROUPS, 2, SUBS, piece, rows), F32),
                 pltpu.VMEM((GROUPS, nz - 1, 2, SUBS, words, rows), jnp.int16),
-                pltpu.VMEM((GROUPS, 2, nz, 8, rows), F32),
+                pltpu.VMEM((GROUPS, 2, nz - 1, 8, rows), F32),
+                pltpu.VMEM((GROUPS, 2, nz - 1, 8, rows), F32),
                 pltpu.VMEM((GROUPS, chunk, rows), F32),
                 pltpu.VMEM((GROUPS, nz, chunk, rows), BF16),
                 pltpu.VMEM((GROUPS, 2, rows, width // 2), F32),
@@ -457,7 +455,7 @@
                 dma((GROUPS, 2)),
                 dma((GROUPS, nz - 1, 2, SUBS)),
                 dma((GROUPS, 2)),
-                dma((GROUPS, nz - 1, 2)),
+                dma((GROUPS, nz - 1, 2, SUBS)),
                 dma((GROUPS,)),
                 dma((GROUPS, nz // 2, 2, 4)),
                 dma((GROUPS, 2)),

time: 148 us -> 141 us (0.953)
  Pallas kernels: 147 us -> 140 us
    pallas_call x1, Pallas kernels: 144 us -> 137 us  [on_device(): pl.pallas_call(functools.partial(kernel, sizes), out_shape=(pltpu.VMEM((n...]
where the time goes in v5:
time: 141 us
  Pallas kernels  140 us (99%)
    pallas_call x1, Pallas kernels, on_device(): pl.pallas_call(functools.partial(kernel, sizes), out_shape=(pltpu.VMEM((n...  137 us
    pallas_call x1, Pallas kernels, on_device(): pl.pallas_call(functools.partial(finish, share), out_shape=(jax.ShapeDtyp...  3.28 us

profile of v5, /device:TPU:1, one launch (start us, length us, event | category | flops | bytes accessed | tf_op | source)
XLA Modules:
  0.0 140.8 jit_solution(979047494428340956)
XLA Ops:
  0.6 136.9 %shard_map.92 = (bf16[8,512,512]{2,1,0:T(8,128)(2,1)S(1)}, f32[8,512,512]{2,1,0:T(8,128)S(1)}, bf16[512,512]{1,0:T(8,128)(2,1)S(1)}, f32[1,512]{1,0:T(1,128)S(1)...) custom-call(bf16[512,512]{1,0:T(8,128)(2,1)} %h_hbm.1, bf16[8,512,512]{2,1,0:T(8,128)(2,1)} %bitcast.8, ...), custom_call_target="tpu_custom_call" | custom-call | flops 6442450944 | bytes 8388608 | tf_op jit(solution)/shard_map/pallas_call | solution.py:419
  137.6 3.3 %shard_map.93 = (bf16[512,512]{1,0:T(8,128)(2,1)}, f32[1,64]{1,0:T(1,128)}, bf16[8,512,512]{2,1,0:T(8,128)(2,1)}, f32[32,128]{1,0:T(8,128)}, f32[1,512]{1,0:T(1,128)}) custom-call(bf16[8,512,512]{2,1,0:T(8,128)(2,1)S(1)} %get-tuple-element.17.w, f32[8,512,512]{2,1,0:T(8,128)S(1)} %get-tuple-element.18.update, bf16[512,512]{1,0:T(8,128)(2,1)S(1)} %get-tuple-element.19.ig_in, ...), custom_call_target="tpu_custom_call" | custom-call | flops 4194304 | bytes 4194304 | tf_op jit(solution)/shard_map/pallas_call | solution.py:479

commit v6 on v5

--- a/solution.py
+++ b/solution.py
@@ -45,24 +45,22 @@
     up, down = {"feat": ring(1)}, {"feat": ring(-1)}
     side = (up, down)
 
+    barrier = pltpu.get_barrier_semaphore()
+
+    def greet(axis, me, n):
+        def body(j, c):
+            pl.semaphore_signal(barrier, inc=1, device_id={axis: lax.rem(me + j, n)}, device_id_type=MESH)
+            return c
+        lax.fori_loop(1, n, body, 0)
+
+    greet("feat", z, nz)
+    greet("cls", cls, nc)
     loads = [pltpu.make_async_copy(h_hbm, h_ref, w_sem.at[nz])]
     loads += [pltpu.make_async_copy(w_hbm.at[o], w.at[o], w_sem.at[o]) for o in range(nz)]
     small = ((target_hbm, target_ref), (rm_hbm, rm_ref), (cm_hbm, cm_ref))
     loads += [pltpu.make_async_copy(a, b, w_sem.at[nz + 1 + i]) for i, (a, b) in enumerate(small)]
     for load in loads:
         load.start()
-
-    barrier = pltpu.get_barrier_semaphore()
-
-    def greet(axis, me, n):
-        def body(j, c):
-            pl.semaphore_signal(barrier, inc=1, device_id={axis: lax.rem(me + j, n)}, device_id_type=MESH)
-            return c
-        lax.fori_loop(1, n, body, 0)
-
-    greet("feat", z, nz)
-    greet("cls", cls, nc)
-    pl.semaphore_wait(barrier, nz - 1 + nc - 1)
     for load in loads:
         load.wait()
 
@@ -99,12 +97,18 @@
         return (high + jnp.concatenate(low, axis=0)).astype(F32) * (top * (1.0 / MOST))
 
     def ring_send(p, s, k, refs, values):
+        ring_write(p, s, k, refs, values)
+        ring_start(p, s, k, refs)
+
+    def ring_write(p, s, k, refs, values):
         tops = [jnp.maximum(jnp.max(jnp.abs(value), axis=0, keepdims=True), 1e-30) for value in values]
         codes = [encode(value, top) for value, top in zip(values, tops)]
         for d in range(2):
             bound[p, d, s, pl.ds(k, 1)] = tops[d]
             refs[d][0:piece, :] = codes[d][0]
             refs[d][piece : piece + piece // PER, :] = codes[d][1]
+
+    def ring_start(p, s, k, refs):
         for d in range(2):
             pltpu.make_async_remote_copy(
                 bound.at[p, d, s, pl.ds(k, 1)], came.at[p, d, s, pl.ds(k, 1)], bd_send.at[p, d], bd_recv.at[p, s, d, k],
@@ -124,7 +128,11 @@
     def rs_first(p):
         value = [partial_logits(p, d, ring(-1) if d == 0 else ring(1)) for d in range(2)]
         for k in range(SUBS):
-            ring_send(p, 0, k, [first.at[p, d, k] for d in range(2)], [value[d][piece * k : piece * (k + 1)] for d in range(2)])
+            ring_write(p, 0, k, [first.at[p, d, k] for d in range(2)], [value[d][piece * k : piece * (k + 1)] for d in range(2)])
+        if p == 0:
+            pl.semaphore_wait(barrier, nz - 1 + nc - 1)
+        for k in range(SUBS):
+            ring_start(p, 0, k, [first.at[p, d, k] for d in range(2)])
 
     def rs_tick(p, s):
         for d in range(2):
@@ -345,7 +353,7 @@
                 carry = carry + square[32 * r : 32 * (r + 1)]
         return carry
 
-    squares = lax.fori_loop(0, 4 * nz, scale, jnp.zeros((32, 128), F32), unroll=2)
+    squares = lax.fori_loop(0, 4 * nz, scale, jnp.zeros((32, 128), F32), unroll=4)
     usum_z[z] = squares[0:8] + squares[8:16] + (squares[16:24] + squares[24:32])
     spread("feat", z, nz, usum_z.at[z], usum_z.at[z], mo_send.at[2], mo_recv.at[2])
     in_sum(1)
@@ -381,23 +389,24 @@
     wait_bytes(usum_c.at[pl.ds(0, nc - 1)], mo_send.at[3])
 
 
-def finish(share, w, update, ig_in, loss_in, nrm_in, ncm_in, factor_ref, ig_ref, loss_ref, nw_hbm, nrm_ref, ncm_ref, new_w, out_sem):
+def finish(share, w, update, ig, loss_in, nrm, ncm, factor_ref, ig_hbm, loss_hbm, nw_hbm, nrm_hbm, ncm_hbm, new_w, loss, out_sem):
     nz, chunk, width = w.shape
     factor = factor_ref[0:1, 0:1]
-    copies = [pltpu.make_async_copy(new_w.at[o], nw_hbm.at[o], out_sem.at[o]) for o in range(nz)]
+    rows = loss_in.shape[1]
+    wide = jnp.broadcast_to(loss_in[...], (8, rows))
+    loss[...] = pltpu.roll(wide, lax.rem(rows - share * lax.axis_index("feat"), rows), 1)[0:1, 0:share]
+    others = ((ig, ig_hbm), (loss, loss_hbm), (nrm, nrm_hbm), (ncm, ncm_hbm))
+    copies = [pltpu.make_async_copy(a, b, out_sem.at[nz + i]) for i, (a, b) in enumerate(others)]
+    for copy in copies:
+        copy.start()
     for o in range(nz):
         def write(k, carry, o=o):
             at = pl.ds(pl.multiple_of(64 * k, 64), 64)
             new_w[o, at, :] = (w[o, at, :].astype(F32) - factor * update[o, at, :]).astype(BF16)
             return carry
         lax.fori_loop(0, chunk // 64, write, 0)
-        copies[o].start()
-    ig_ref[...] = ig_in[...]
-    rows = loss_in.shape[1]
-    loss = jnp.broadcast_to(loss_in[...], (8, rows))
-    loss_ref[...] = pltpu.roll(loss, lax.rem(rows - share * lax.axis_index("feat"), rows), 1)[0:1, 0:share]
-    nrm_ref[...] = nrm_in[...]
-    ncm_ref[...] = ncm_in[...]
+        copies.append(pltpu.make_async_copy(new_w.at[o], nw_hbm.at[o], out_sem.at[o]))
+        copies[-1].start()
     for copy in copies:
         copy.wait()
 
@@ -486,8 +495,8 @@
                 jax.ShapeDtypeStruct((1, width), F32),
             ),
             in_specs=[vmem] * 7,
-            out_specs=(vmem, vmem, hbm, vmem, vmem),
-            scratch_shapes=[pltpu.VMEM((nz, chunk, width), BF16), dma((nz,))],
+            out_specs=(hbm,) * 5,
+            scratch_shapes=[pltpu.VMEM((nz, chunk, width), BF16), pltpu.VMEM((1, share), F32), dma((nz + 4,))],
             compiler_params=pltpu.CompilerParams(vmem_limit_bytes=36 * 2**20),
             cost_estimate=pl.CostEstimate(flops=2 * classes * width, bytes_accessed=2 * classes * width, transcendentals=0),
         )(*between)

time: 141 us -> 139 us (0.986)
  no operation moved by 1% of the time
where the time goes in v6:
time: 139 us
  Pallas kernels  139 us (100%)
    pallas_call x1, Pallas kernels, on_device(): pl.pallas_call(functools.partial(kernel, sizes), out_shape=(pltpu.VMEM((n...  136 us

profile of v6, /device:TPU:1, one launch (start us, length us, event | category | flops | bytes accessed | tf_op | source)
XLA Modules:
  0.0 139.1 jit_solution(16762434668220048758)
XLA Ops:
  0.6 135.9 %shard_map.92 = (bf16[8,512,512]{2,1,0:T(8,128)(2,1)S(1)}, f32[8,512,512]{2,1,0:T(8,128)S(1)}, bf16[512,512]{1,0:T(8,128)(2,1)S(1)}, f32[1,512]{1,0:T(1,128)S(1)...) custom-call(bf16[512,512]{1,0:T(8,128)(2,1)} %h_hbm.1, bf16[8,512,512]{2,1,0:T(8,128)(2,1)} %bitcast.8, ...), custom_call_target="tpu_custom_call" | custom-call | flops 6442450944 | bytes 8388608 | tf_op jit(solution)/shard_map/pallas_call | solution.py:428
  136.6 2.6 %shard_map.93 = (bf16[512,512]{1,0:T(8,128)(2,1)}, f32[1,64]{1,0:T(1,128)}, bf16[8,512,512]{2,1,0:T(8,128)(2,1)}, f32[32,128]{1,0:T(8,128)}, f32[1,512]{1,0:T(1,128)}) custom-call(bf16[8,512,512]{2,1,0:T(8,128)(2,1)S(1)} %get-tuple-element.17.w, f32[8,512,512]{2,1,0:T(8,128)S(1)} %get-tuple-element.18.update, bf16[512,512]{1,0:T(8,128)(2,1)S(1)} %get-tuple-element.19.ig, ...), custom_call_target="tpu_custom_call" | custom-call | flops 4194304 | bytes 4194304 | tf_op jit(solution)/shard_map/pallas_call | solution.py:488
